TPU v7x, 512 devices: a whole 4x4x16 slice. The times are simulated.
512 devices in a mesh: ctx: 64 (over z, x), grp: 8 (over y, core).
Axes of the slice: x: 4, y: 4, z: 16, core: 2. Of those that a mesh axis runs over, the one named last changes fastest.
Arguments:
- queries: bfloat16 [8, 16384, 2560], P('grp', 'ctx'), may hold values from -8 to 8
- keys: bfloat16 [8, 16384, 512], P('grp', 'ctx'), may hold values from -6 to 6
- values: bfloat16 [8, 16384, 512], P('grp', 'ctx'), may hold values from -6 to 6
- upstream: bfloat16 [8, 16384, 2560], P('grp', 'ctx'), may hold values from -6 to 6
- lengths: int32 [8, 64], P('grp'), may hold values from 1 to 512, 16384 in all within a row
- group_ids: int32 [8, 64], P('grp'), may hold values from 0 to 31
- rewards: float32 [8, 64], P('grp'), may hold values from -4 to 4
Outputs:
- query_grad: bfloat16 [8, 16384, 2560], P('grp', 'ctx')
- key_grad: bfloat16 [8, 16384, 512], P('grp', 'ctx')
- value_grad: bfloat16 [8, 16384, 512], P('grp', 'ctx')
Inputs may be any that keep to these rules, and one draw needn't show every extreme that they name: Each row's lengths sum to 16384; in every row the longest trajectory has exactly 512 positions.
All inputs are finite; a program needn't handle non-finite values.
Results may differ from a plain program's by a relative error of at most 0.02.
Values may be sent and summed in bfloat16 or wider, within the bound.
No kernel may reach another device: no remote copies, remote signals or barrier semaphores. Data moves between devices by JAX's collectives and lax.ppermute only.
A program may use at most 64 MiB of HBM per device.

v0:
```python
import math

import jax
import jax.numpy as jnp
from jax import lax
from jax.sharding import PartitionSpec as P

QH = 20
KVH = 4
HEAD = 128
SPAN = 2
GRP_ROW = 4


def shifted(x, axis, by):
    length = lax.axis_size(axis)
    pairs = [(i, i + by) for i in range(length) if 0 <= i + by < length]
    return lax.ppermute(x, axis, pairs)


def segment_of(starts, positions):
    return jnp.sum((positions[:, None] >= starts[None, :]).astype(jnp.int32), axis=1) - 1


def group_backward(query_part, key_part, value_part, weighted_part, allowed):
    score_scale = 1.0 / math.sqrt(key_part.shape[-1])
    scores = (
        jnp.einsum("tjd,sd->jts", query_part, key_part, preferred_element_type=jnp.float32)
        * score_scale
    )
    scores = jnp.where(allowed[None], scores, -jnp.inf)
    row_max = jnp.max(scores, axis=2, keepdims=True)
    log_total = row_max + jnp.log(jnp.sum(jnp.exp(scores - row_max), axis=2, keepdims=True))
    soft_weights = jnp.exp(scores - log_total).astype(jnp.bfloat16)
    attended = jnp.einsum(
        "jts,sd->tjd", soft_weights, value_part, preferred_element_type=jnp.float32
    ).astype(jnp.bfloat16)
    delta_sum = jnp.sum(weighted_part.astype(jnp.float32) * attended.astype(jnp.float32), axis=2)
    grad_soft = jnp.einsum(
        "tjd,sd->jts", weighted_part, value_part, preferred_element_type=jnp.float32
    )
    grad_score = (
        soft_weights.astype(jnp.float32)
        * (grad_soft - jnp.transpose(delta_sum)[:, :, None])
        * score_scale
    ).astype(jnp.bfloat16)
    query_grad = jnp.einsum(
        "jts,sd->tjd", grad_score, key_part, preferred_element_type=jnp.float32
    ).astype(jnp.bfloat16)
    key_grad = jnp.einsum("jts,tjd->sd", grad_score, query_part, preferred_element_type=jnp.float32)
    value_grad = jnp.einsum(
        "jts,tjd->sd", soft_weights, weighted_part, preferred_element_type=jnp.float32
    )
    return (query_grad, key_grad, value_grad)


def local(queries, keys, values, upstream, lengths, group_ids, rewards):
    rows_here = queries.shape[1]
    width_kv = keys.shape[2]
    per_group = QH // KVH
    groups_all = GRP_ROW * lax.axis_size("grp")
    row_lengths = lengths[0]
    row_rewards = rewards[0]
    member = group_ids[0][:, None] == jnp.arange(groups_all, dtype=jnp.int32)[None, :]
    local_sums = jnp.sum(jnp.where(member, row_rewards[:, None], 0.0), axis=0)
    local_counts = jnp.sum(member.astype(jnp.float32), axis=0)
    group_sums, group_counts = lax.psum((local_sums, local_counts), "grp")
    own_sum = jnp.sum(jnp.where(member, group_sums[None, :], 0.0), axis=1)
    own_count = jnp.sum(jnp.where(member, group_counts[None, :], 0.0), axis=1)
    advantage = row_rewards - (own_sum - row_rewards) / jnp.maximum(own_count - 1.0, 1.0)
    starts = jnp.cumsum(row_lengths) - row_lengths
    first_row = lax.axis_index("ctx") * rows_here
    query_pos = first_row + jnp.arange(rows_here, dtype=jnp.int32)
    query_seg = segment_of(starts, query_pos)
    picked = query_seg[:, None] == jnp.arange(row_lengths.shape[0], dtype=jnp.int32)[None, :]
    token_weight = jnp.sum(jnp.where(picked, advantage[None, :], 0.0), axis=1)
    weighted = (upstream[0].astype(jnp.float32) * token_weight[:, None]).astype(jnp.bfloat16)
    paired = jnp.concatenate([keys[0], values[0]], axis=1)
    earlier = [shifted(paired, "ctx", distance) for distance in range(SPAN, 0, -1)]
    window = jnp.concatenate(earlier + [paired], axis=0)
    span_rows = window.shape[0]
    key_window = window[:, :width_kv]
    value_window = window[:, width_kv:]
    key_pos = first_row - SPAN * rows_here + jnp.arange(span_rows, dtype=jnp.int32)
    key_seg = segment_of(starts, key_pos)
    allowed = (
        (key_seg[None, :] == query_seg[:, None])
        & (key_pos[None, :] <= query_pos[:, None])
        & (key_pos[None, :] >= 0)
    )
    query_split = jnp.moveaxis(queries[0].reshape(rows_here, KVH, per_group, HEAD), 1, 0)
    weighted_split = jnp.moveaxis(weighted.reshape(rows_here, KVH, per_group, HEAD), 1, 0)
    key_split = jnp.moveaxis(key_window.reshape(span_rows, KVH, HEAD), 1, 0)
    value_split = jnp.moveaxis(value_window.reshape(span_rows, KVH, HEAD), 1, 0)
    query_grad, key_grad, value_grad = lax.map(
        lambda group_items: group_backward(
            group_items[0], group_items[1], group_items[2], group_items[3], allowed
        ),
        (query_split, key_split, value_split, weighted_split),
    )
    query_grad = jnp.moveaxis(query_grad, 0, 1).reshape(rows_here, QH * HEAD)
    key_grad = jnp.moveaxis(key_grad, 0, 1).reshape(span_rows, width_kv)
    value_grad = jnp.moveaxis(value_grad, 0, 1).reshape(span_rows, width_kv)
    partials = jnp.concatenate([key_grad, value_grad], axis=1).reshape(
        SPAN + 1, rows_here, 2 * width_kv
    )
    summed = partials[SPAN]
    for distance in range(1, SPAN + 1):
        summed = summed + shifted(partials[SPAN - distance], "ctx", -distance)
    key_out = summed[:, :width_kv].astype(jnp.bfloat16)
    value_out = summed[:, width_kv:].astype(jnp.bfloat16)
    return (query_grad[None], key_out[None], value_out[None])


def solution(mesh):
    in_specs = (
        P("grp", "ctx", None),
        P("grp", "ctx", None),
        P("grp", "ctx", None),
        P("grp", "ctx", None),
        P("grp", None),
        P("grp", None),
        P("grp", None),
    )
    out_specs = (P("grp", "ctx", None), P("grp", "ctx", None), P("grp", "ctx", None))
    return jax.shard_map(local, mesh=mesh, in_specs=in_specs, out_specs=out_specs, check_vma=False)
```

profile of v0, /device:TPU:268, one launch (start us, length us, event | category | flops | bytes accessed | tf_op | source)
XLA Modules:
  0.0 172.3 jit_solution(13239457920047797658)
XLA Ops:
  3.8 2.9 %collective-permute-start = (bf16[256,1024]{0,1:T(8,128)(2,1)}, bf16[256,1024]{0,1:T(8,128)(2,1)}, u32[]{:S(2)}, u32[]{:S(2)}) collective-permute-start(bf16[256,1024]{0,1:T(8,128)(2,1)} %pad_maximum_fusion), channel_id=1, source_target_pairs={{0,16},{8,24},{16,32},{24,40},{32,48},{40,56},{48,64},{56,72},{64,... | collective-permute-start | bytes 1572872 | tf_op jit(solution)/shard_map/ppermute | solution.py:18
  6.7 4.0 %collective-permute-start.1 = (bf16[256,1024]{0,1:T(8,128)(2,1)}, bf16[256,1024]{0,1:T(8,128)(2,1)}, u32[]{:S(2)}, u32[]{:S(2)}) collective-permute-start(bf16[256,1024]{0,1:T(8,128)(2,1)} %pad_maximum_fusion), channel_id=1, source_target_pairs={{0,8},{8,16},{16,24},{24,32},{32,40},{40,48},{48,56},{56,64},{64,7... | collective-permute-start | bytes 1572872 | tf_op jit(solution)/shard_map/ppermute | solution.py:18
  11.3 11.5 %all-reduce = (f32[32]{0:T(128)S(1)}, f32[32]{0:T(128)S(1)}) all-reduce(f32[32]{0:T(128)S(1)} %get-tuple-element.122, f32[32]{0:T(128)S(1)} %get-tuple-element.123), channel_id=1, replica_groups=mesh['ctx'=64,'grp'=8] {'grp'}, use_global_device_ids=true, to_apply=%region_3.4 | all-reduce | flops 64 | bytes 512 | tf_op jit(solution)/shard_map/psum | solution.py:67
  23.7 2.4 %copy.41 = bf16[1,256,2560]{1,2,0:T(8,128)(2,1)} copy(bf16[1,256,2560]{2,1,0:T(8,128)(2,1)} %param.9) | data formatting | bytes 2621440 | tf_op args[0]
  27.5 4.9 %collective-permute-done.1 = bf16[256,1024]{0,1:T(8,128)(2,1)} collective-permute-done((bf16[256,1024]{0,1:T(8,128)(2,1)}, bf16[256,1024]{0,1:T(8,128)(2,1)}, u32[]{:S(2)}, u32[]{:S(2)}) %collective-permute-start.1) | collective-permute-done | bytes 524320 | tf_op jit(solution)/shard_map/ppermute | solution.py:18
  34.7 56.7 %while.15 = (s32[]{:T(128)}, bf16[4,256,5,128]{1,3,2,0:T(8,128)(2,1)}, f32[4,768,128]{2,1,0:T(8,128)}, f32[4,768,128]{2,1,0:T(8,128)}, bf16[4,768,128]{1,2,0:T(8...) while((s32[]{:T(128)}, ...), condition=%wide.region_14.15_spmd.clone, body=%wide.region_10.14_spmd.clone.sunk | while | flops 1527444992 | bytes 36501924 | solution.py:95
  35.4 1.8 %fusion.74 = (f32[5,256]{1,0:T(8,128)S(1)}, f32[768,256,5]{1,0,2:T(8,128)S(1)}) fusion(pred[256,768]{0,1:T(8,128)(4,1)S(1)} %and_and_fusion.2, bf16[4,256,5,128]{1,3,2,0:T(8,128)(2,1)} %get-tuple-element.276, s32[]{:T(128)} %get-tuple-element.257, bf16[4,768,128]{1,2,0:T(8,128)(2,1)S(1)} %get-tuple-element.275), kind=kOutput, calls=%fused_computation.8.clone.1 | convolution fusion | flops 254606080 | bytes 4659200 | tf_op jit(solution)/shard_map/while/body/eval_jaxpr/tjd,sd->jts/dot_general | solution.py:28
  40.1 2.0 %fusion.75 = f32[256,5]{0,1:T(8,128)S(1)} fusion(bf16[5,256,768]{1,2,0:T(8,128)(2,1)S(1)} %exponential_convert_fusion.2, bf16[1,256,5,128]{3,1,2,0:T(8,128)(2,1)S(1)} %copy.66, bf16[4,768,128]{1,2,0:T(8,128)(2,1)} %get-tuple-element.277, s32[]{:T(128)} %get-tuple-element.257), kind=kOutput, calls=%fused_computation.18.clone.1 | convolution fusion | flops 252476160 | bytes 2496000 | tf_op jit(solution)/shard_map/while/body/eval_jaxpr/jts,sd->tjd/dot_general | solution.py:35
  42.1 1.7 fusion.76
  43.9 2.4 %fusion.78 = f32[4,768,128]{2,1,0:T(8,128)} fusion(f32[4,768,128]{2,1,0:T(8,128)} %get-tuple-element.259, s32[]{:T(128)} %get-tuple-element.257, bf16[5,256,768]{1,2,0:T(8,128)(2,1)S(1)} %fusion.76, bf16[4,256,5,128]{1,3,2,0:T(8,128)(2,1)} %get-tuple-element.276), kind=kOutput, calls=%fused_computation.17.clone.1 | convolution fusion | flops 251658240 | bytes 2688000 | tf_op jit(solution)/shard_map/while/body/eval_jaxpr/jts,tjd->sd/dot_general | solution.py:50
  49.6 1.8 %fusion.74 = (f32[5,256]{1,0:T(8,128)S(1)}, f32[768,256,5]{1,0,2:T(8,128)S(1)}) fusion(pred[256,768]{0,1:T(8,128)(4,1)S(1)} %and_and_fusion.2, bf16[4,256,5,128]{1,3,2,0:T(8,128)(2,1)} %get-tuple-element.276, s32[]{:T(128)} %get-tuple-element.257, bf16[4,768,128]{1,2,0:T(8,128)(2,1)S(1)} %get-tuple-element.275), kind=kOutput, calls=%fused_computation.8.clone.1 | convolution fusion | flops 254606080 | bytes 4659200 | tf_op jit(solution)/shard_map/while/body/eval_jaxpr/tjd,sd->jts/dot_general | solution.py:28
  54.2 2.0 %fusion.75 = f32[256,5]{0,1:T(8,128)S(1)} fusion(bf16[5,256,768]{1,2,0:T(8,128)(2,1)S(1)} %exponential_convert_fusion.2, bf16[1,256,5,128]{3,1,2,0:T(8,128)(2,1)S(1)} %copy.66, bf16[4,768,128]{1,2,0:T(8,128)(2,1)} %get-tuple-element.277, s32[]{:T(128)} %get-tuple-element.257), kind=kOutput, calls=%fused_computation.18.clone.1 | convolution fusion | flops 252476160 | bytes 2496000 | tf_op jit(solution)/shard_map/while/body/eval_jaxpr/jts,sd->tjd/dot_general | solution.py:35
  56.3 1.7 fusion.76
  58.0 2.4 %fusion.78 = f32[4,768,128]{2,1,0:T(8,128)} fusion(f32[4,768,128]{2,1,0:T(8,128)} %get-tuple-element.259, s32[]{:T(128)} %get-tuple-element.257, bf16[5,256,768]{1,2,0:T(8,128)(2,1)S(1)} %fusion.76, bf16[4,256,5,128]{1,3,2,0:T(8,128)(2,1)} %get-tuple-element.276), kind=kOutput, calls=%fused_computation.17.clone.1 | convolution fusion | flops 251658240 | bytes 2688000 | tf_op jit(solution)/shard_map/while/body/eval_jaxpr/jts,tjd->sd/dot_general | solution.py:50
  61.6 1.5 fusion.79
  63.8 1.8 %fusion.74 = (f32[5,256]{1,0:T(8,128)S(1)}, f32[768,256,5]{1,0,2:T(8,128)S(1)}) fusion(pred[256,768]{0,1:T(8,128)(4,1)S(1)} %and_and_fusion.2, bf16[4,256,5,128]{1,3,2,0:T(8,128)(2,1)} %get-tuple-element.276, s32[]{:T(128)} %get-tuple-element.257, bf16[4,768,128]{1,2,0:T(8,128)(2,1)S(1)} %get-tuple-element.275), kind=kOutput, calls=%fused_computation.8.clone.1 | convolution fusion | flops 254606080 | bytes 4659200 | tf_op jit(solution)/shard_map/while/body/eval_jaxpr/tjd,sd->jts/dot_general | solution.py:28
  68.4 2.0 %fusion.75 = f32[256,5]{0,1:T(8,128)S(1)} fusion(bf16[5,256,768]{1,2,0:T(8,128)(2,1)S(1)} %exponential_convert_fusion.2, bf16[1,256,5,128]{3,1,2,0:T(8,128)(2,1)S(1)} %copy.66, bf16[4,768,128]{1,2,0:T(8,128)(2,1)} %get-tuple-element.277, s32[]{:T(128)} %get-tuple-element.257), kind=kOutput, calls=%fused_computation.18.clone.1 | convolution fusion | flops 252476160 | bytes 2496000 | tf_op jit(solution)/shard_map/while/body/eval_jaxpr/jts,sd->tjd/dot_general | solution.py:35
  70.5 1.7 fusion.76
  72.2 2.4 %fusion.78 = f32[4,768,128]{2,1,0:T(8,128)} fusion(f32[4,768,128]{2,1,0:T(8,128)} %get-tuple-element.259, s32[]{:T(128)} %get-tuple-element.257, bf16[5,256,768]{1,2,0:T(8,128)(2,1)S(1)} %fusion.76, bf16[4,256,5,128]{1,3,2,0:T(8,128)(2,1)} %get-tuple-element.276), kind=kOutput, calls=%fused_computation.17.clone.1 | convolution fusion | flops 251658240 | bytes 2688000 | tf_op jit(solution)/shard_map/while/body/eval_jaxpr/jts,tjd->sd/dot_general | solution.py:50
  77.9 1.8 %fusion.74 = (f32[5,256]{1,0:T(8,128)S(1)}, f32[768,256,5]{1,0,2:T(8,128)S(1)}) fusion(pred[256,768]{0,1:T(8,128)(4,1)S(1)} %and_and_fusion.2, bf16[4,256,5,128]{1,3,2,0:T(8,128)(2,1)} %get-tuple-element.276, s32[]{:T(128)} %get-tuple-element.257, bf16[4,768,128]{1,2,0:T(8,128)(2,1)S(1)} %get-tuple-element.275), kind=kOutput, calls=%fused_computation.8.clone.1 | convolution fusion | flops 254606080 | bytes 4659200 | tf_op jit(solution)/shard_map/while/body/eval_jaxpr/tjd,sd->jts/dot_general | solution.py:28
  82.6 2.0 %fusion.75 = f32[256,5]{0,1:T(8,128)S(1)} fusion(bf16[5,256,768]{1,2,0:T(8,128)(2,1)S(1)} %exponential_convert_fusion.2, bf16[1,256,5,128]{3,1,2,0:T(8,128)(2,1)S(1)} %copy.66, bf16[4,768,128]{1,2,0:T(8,128)(2,1)} %get-tuple-element.277, s32[]{:T(128)} %get-tuple-element.257), kind=kOutput, calls=%fused_computation.18.clone.1 | convolution fusion | flops 252476160 | bytes 2496000 | tf_op jit(solution)/shard_map/while/body/eval_jaxpr/jts,sd->tjd/dot_general | solution.py:35
  84.6 1.7 fusion.76
  86.3 2.4 %fusion.78 = f32[4,768,128]{2,1,0:T(8,128)} fusion(f32[4,768,128]{2,1,0:T(8,128)} %get-tuple-element.259, s32[]{:T(128)} %get-tuple-element.257, bf16[5,256,768]{1,2,0:T(8,128)(2,1)S(1)} %fusion.76, bf16[4,256,5,128]{1,3,2,0:T(8,128)(2,1)} %get-tuple-element.276), kind=kOutput, calls=%fused_computation.17.clone.1 | convolution fusion | flops 251658240 | bytes 2688000 | tf_op jit(solution)/shard_map/while/body/eval_jaxpr/jts,tjd->sd/dot_general | solution.py:50
  91.4 1.6 bitcast_dynamic-update-slice_fusion.1
  93.0 1.6 bitcast_dynamic-update-slice_fusion
  94.6 1.5 fusion.40
  96.1 2.5 %collective-permute-start.2 = (f32[256,1024]{1,0:T(8,128)}, f32[256,1024]{1,0:T(8,128)}, u32[]{:S(2)}, u32[]{:S(2)}) collective-permute-start(f32[256,1024]{1,0:T(8,128)} %get-tuple-element.154), channel_id=1, source_target_pairs={{8,0},{16,8},{24,16},{32,24},{40,32},{48,40},{56,48},{64,56},{72,6... | collective-permute-start | bytes 3145736 | tf_op jit(solution)/shard_map/ppermute | solution.py:18
  98.6 4.6 %collective-permute-start.3 = (f32[256,1024]{1,0:T(8,128)}, f32[256,1024]{1,0:T(8,128)}, u32[]{:S(2)}, u32[]{:S(2)}) collective-permute-start(f32[256,1024]{1,0:T(8,128)} %get-tuple-element.155), channel_id=1, source_target_pairs={{16,0},{24,8},{32,16},{40,24},{48,32},{56,40},{64,48},{72,56},{80,... | collective-permute-start | bytes 3145736 | tf_op jit(solution)/shard_map/ppermute | solution.py:18
  103.2 2.4 %copy.49 = bf16[1,256,2560]{2,1,0:T(8,128)(2,1)} copy(bf16[1,256,2560]{1,2,0:T(8,128)(2,1)} %bitcast.185) | data formatting | bytes 2621440
  105.6 18.7 %collective-permute-done.2 = f32[256,1024]{1,0:T(8,128)} collective-permute-done((f32[256,1024]{1,0:T(8,128)}, f32[256,1024]{1,0:T(8,128)}, u32[]{:S(2)}, u32[]{:S(2)}) %collective-permute-start.2) | collective-permute-done | bytes 1048608 | tf_op jit(solution)/shard_map/ppermute | solution.py:18
  124.3 45.4 %collective-permute-done.3 = f32[256,1024]{1,0:T(8,128)} collective-permute-done((f32[256,1024]{1,0:T(8,128)}, f32[256,1024]{1,0:T(8,128)}, u32[]{:S(2)}, u32[]{:S(2)}) %collective-permute-start.3) | collective-permute-done | bytes 1048608 | tf_op jit(solution)/shard_map/ppermute | solution.py:18
  169.7 1.8 %fusion.37 = bf16[256,1024]{1,0:T(8,128)(2,1)S(1)} fusion(f32[256,1024]{1,0:T(8,128)} %collective-permute-done.3, f32[256,1024]{1,0:T(8,128)} %collective-permute-done.2, f32[768,1024]{1,0:T(8,128)S(1)} %bitcast_dynamic-update-slice_fusion), kind=kLoop, calls=%fused_computation.52 | loop fusion | flops 786432 | bytes 3670016 | tf_op jit(solution)/shard_map/convert.3
  (72 shorter events, 32.1 us)
Async XLA Ops:
  0.6 10.1 %copy-start.4 = (s32[1,64]{1,0:T(1,128)S(1)}, s32[1,64]{1,0:T(1,128)}, u32[]{:S(2)}) copy-start(s32[1,64]{1,0:T(1,128)} %param.13) | copy-start | bytes 772
  0.6 10.5 %copy-start.2 = (s32[1,64]{1,0:T(1,128)S(1)}, s32[1,64]{1,0:T(1,128)}, u32[]{:S(2)}) copy-start(s32[1,64]{1,0:T(1,128)} %param.14) | copy-start | bytes 772
  0.7 10.5 %copy-start.3 = (f32[1,64]{1,0:T(1,128)S(1)}, f32[1,64]{1,0:T(1,128)}, u32[]{:S(2)}) copy-start(f32[1,64]{1,0:T(1,128)} %param.15) | copy-start | bytes 772
  0.7 22.4 %copy-start.1 = (bf16[1,256,2560]{2,1,0:T(8,128)(2,1)S(1)}, bf16[1,256,2560]{2,1,0:T(8,128)(2,1)}, u32[]{:S(2)}) copy-start(bf16[1,256,2560]{2,1,0:T(8,128)(2,1)} %param.12) | copy-start | bytes 3932164
  3.8 23.7 %collective-permute-start = (bf16[256,1024]{0,1:T(8,128)(2,1)}, bf16[256,1024]{0,1:T(8,128)(2,1)}, u32[]{:S(2)}, u32[]{:S(2)}) collective-permute-start(bf16[256,1024]{0,1:T(8,128)(2,1)} %pad_maximum_fusion), channel_id=1, source_target_pairs={{0,16},{8,24},{16,32},{24,40},{32,48},{40,56},{48,64},{56,72},{64,... | collective-permute-start | bytes 1572872 | tf_op jit(solution)/shard_map/ppermute | solution.py:18
  6.7 25.7 %collective-permute-start.1 = (bf16[256,1024]{0,1:T(8,128)(2,1)}, bf16[256,1024]{0,1:T(8,128)(2,1)}, u32[]{:S(2)}, u32[]{:S(2)}) collective-permute-start(bf16[256,1024]{0,1:T(8,128)(2,1)} %pad_maximum_fusion), channel_id=1, source_target_pairs={{0,8},{8,16},{16,24},{24,32},{32,40},{40,48},{48,56},{56,64},{64,7... | collective-permute-start | bytes 1572872 | tf_op jit(solution)/shard_map/ppermute | solution.py:18
  40.1 2.1 %copy-start = (bf16[4,256,5,128]{1,3,2,0:T(8,128)(2,1)S(1)}, bf16[4,256,5,128]{1,3,2,0:T(8,128)(2,1)}, u32[]{:S(2)}) copy-start(bf16[4,256,5,128]{1,3,2,0:T(8,128)(2,1)} %get-tuple-element.278) | copy-start | bytes 3932164 | tf_op jit(solution)/shard_map/while
  54.2 2.1 %copy-start = (bf16[4,256,5,128]{1,3,2,0:T(8,128)(2,1)S(1)}, bf16[4,256,5,128]{1,3,2,0:T(8,128)(2,1)}, u32[]{:S(2)}) copy-start(bf16[4,256,5,128]{1,3,2,0:T(8,128)(2,1)} %get-tuple-element.278) | copy-start | bytes 3932164 | tf_op jit(solution)/shard_map/while
  68.4 2.1 %copy-start = (bf16[4,256,5,128]{1,3,2,0:T(8,128)(2,1)S(1)}, bf16[4,256,5,128]{1,3,2,0:T(8,128)(2,1)}, u32[]{:S(2)}) copy-start(bf16[4,256,5,128]{1,3,2,0:T(8,128)(2,1)} %get-tuple-element.278) | copy-start | bytes 3932164 | tf_op jit(solution)/shard_map/while
  82.6 2.1 %copy-start = (bf16[4,256,5,128]{1,3,2,0:T(8,128)(2,1)S(1)}, bf16[4,256,5,128]{1,3,2,0:T(8,128)(2,1)}, u32[]{:S(2)}) copy-start(bf16[4,256,5,128]{1,3,2,0:T(8,128)(2,1)} %get-tuple-element.278) | copy-start | bytes 3932164 | tf_op jit(solution)/shard_map/while
  96.1 28.2 %collective-permute-start.2 = (f32[256,1024]{1,0:T(8,128)}, f32[256,1024]{1,0:T(8,128)}, u32[]{:S(2)}, u32[]{:S(2)}) collective-permute-start(f32[256,1024]{1,0:T(8,128)} %get-tuple-element.154), channel_id=1, source_target_pairs={{8,0},{16,8},{24,16},{32,24},{40,32},{48,40},{56,48},{64,56},{72,6... | collective-permute-start | bytes 3145736 | tf_op jit(solution)/shard_map/ppermute | solution.py:18
  98.6 71.1 %collective-permute-start.3 = (f32[256,1024]{1,0:T(8,128)}, f32[256,1024]{1,0:T(8,128)}, u32[]{:S(2)}, u32[]{:S(2)}) collective-permute-start(f32[256,1024]{1,0:T(8,128)} %get-tuple-element.155), channel_id=1, source_target_pairs={{16,0},{24,8},{32,16},{40,24},{48,32},{56,40},{64,48},{72,56},{80,... | collective-permute-start | bytes 3145736 | tf_op jit(solution)/shard_map/ppermute | solution.py:18
where the time goes:
time: 173 us; the launch traced here: 172 us
  waiting for transfers between devices  69 us (40%)
  matrix products  42.2 us (24%)
  local copies, waits for them, and re-layouts  19.1 us (11%)
  other arithmetic  15.4 us (9%)
  starting transfers between devices  13.9 us (8%)
  blocking collectives  11.5 us (7%)
    ppermute x4, waiting for transfers between devices, shifted(): return lax.ppermute(x, axis, pairs)  69 us
    ppermute x4, starting transfers between devices, shifted(): return lax.ppermute(x, axis, pairs)  13.9 us
    psum x1, blocking collectives, local(): group_sums, group_counts = lax.psum((local_sums, local_counts), 'grp')  11.5 us
    dot_general x4, matrix products, group_backward(): jnp.einsum('jts,tjd->sd', grad_score, query_part, preferred_element_type=...  9.62 us
    unnamed x14, local copies, waits for them, and re-layouts  9.36 us
    dot_general x4, matrix products, group_backward(): jnp.einsum('jts,sd->tjd', soft_weights, value_part, preferred_element_typ...  8.16 us
    dot_general x4, matrix products, group_backward(): jnp.einsum('tjd,sd->jts', query_part, key_part, preferred_element_type=jn...  7.16 us
    dot_general x4, matrix products, group_backward(): jnp.einsum('tjd,sd->jts', weighted_part, value_part, preferred_element_ty...  6.85 us
  transfers between devices with their start and end apart: 4, of which 3 were waited for; matrix products, arithmetic and copies ran while one was open for 4% of the time, Pallas kernels for 0%

commit v1 on v0

v1 whole, which is shorter than its diff:
```python
import math

import jax
import jax.numpy as jnp
from jax import lax
from jax.experimental import pallas as pl
from jax.experimental.pallas import tpu as pltpu
from jax.sharding import PartitionSpec as P

QH = 20
KVH = 4
HEAD = 128
SPAN = 2
GRP_ROW = 4
PER = QH // KVH
HALF = 128
ROWS = 256
REACH = 640
WINDOW = 768
SCALE = 1.0 / math.sqrt(HEAD)
EXP_SCALE = SCALE * math.log2(math.e)
EXCLUDED = -1e30


def shifted(x, axis, by):
    length = lax.axis_size(axis)
    pairs = [(i, i + by) for i in range(length) if 0 <= i + by < length]
    return lax.ppermute(x, axis, pairs)


def attention_kernel(
    low_ref, gain_ref, q_ref, u_ref, k_ref, v_ref, near_ref, far_ref,
    dq_ref, own_ref, to_near_ref, to_far_ref,
    mask, kw, vw, kt, qj, uj, s, uv, p, ds, dk, dv,
):
    f32, bf16 = jnp.float32, jnp.bfloat16

    @pl.when(pl.program_id(0) == 0)
    def _():
        for j in range(2):
            key_at = lax.broadcasted_iota(jnp.int32, (REACH, HALF), 0) + j * HALF
            query_at = lax.broadcasted_iota(jnp.int32, (REACH, HALF), 1) + (SPAN * ROWS + j * HALF)
            low = low_ref[:, j * HALF : (j + 1) * HALF]
            mask[j] = jnp.where((key_at <= query_at) & (key_at >= low), 0.0, EXCLUDED).astype(f32)

    for window, at, own in ((kw, 0, k_ref), (vw, 1, v_ref)):
        window[0:ROWS] = far_ref[at]
        window[ROWS : 2 * ROWS] = near_ref[at]
        window[2 * ROWS :] = own[...]
    kt[...] = kw[...].T
    dk[...] = jnp.zeros_like(dk)
    dv[...] = jnp.zeros_like(dv)
    for j in range(2):
        first = j * HALF
        rows = slice(first, first + HALF)
        keys = slice(first, first + REACH)
        for h in range(PER):
            cols = slice(h * HEAD, (h + 1) * HEAD)
            qj[h * HALF : (h + 1) * HALF] = q_ref[rows, cols]
            uj[h * HALF : (h + 1) * HALF] = u_ref[rows, cols]
        inner = (((1,), (1,)), ((), ()))
        s[...] = lax.dot_general(kw[keys], qj[...], inner, preferred_element_type=f32)
        uv[...] = lax.dot_general(vw[keys], uj[...], inner, preferred_element_type=f32)
        for h in range(PER):
            lanes = slice(h * HALF, (h + 1) * HALF)
            tiles = [slice(t * HALF, (t + 1) * HALF) for t in range(REACH // HALF)]
            top = None
            for tile in tiles:
                x = s[tile, lanes] + mask[j, tile]
                s[tile, lanes] = x
                part = jnp.max(x.reshape(HALF // 8, 8, HALF), axis=0)
                top = part if top is None else jnp.maximum(top, part)
            top = jnp.max(top, axis=0, keepdims=True)
            total = inner_sum = None
            for tile in tiles:
                e = jnp.exp2((s[tile, lanes] - top) * EXP_SCALE)
                s[tile, lanes] = e
                part = jnp.sum(e.reshape(HALF // 8, 8, HALF), axis=0)
                part_uv = jnp.sum((e * uv[tile, lanes]).reshape(HALF // 8, 8, HALF), axis=0)
                total = part if total is None else total + part
                inner_sum = part_uv if inner_sum is None else inner_sum + part_uv
            inverse = 1.0 / jnp.sum(total, axis=0, keepdims=True)
            delta = jnp.sum(inner_sum, axis=0, keepdims=True) * inverse
            for tile in tiles:
                soft = s[tile, lanes] * inverse
                p[tile, lanes] = soft.astype(bf16)
                ds[tile, lanes] = (soft * (uv[tile, lanes] - delta)).astype(bf16)
        dv[keys] += jnp.dot(p[...], uj[...], preferred_element_type=f32)
        dk[keys] += jnp.dot(ds[...], qj[...], preferred_element_type=f32)
        dq_t = jnp.dot(kt[:, keys], ds[...], preferred_element_type=f32)
        gain = gain_ref[:, rows]
        for h in range(PER):
            block = dq_t[:, h * HALF : (h + 1) * HALF] * gain
            dq_ref[rows, h * HEAD : (h + 1) * HEAD] = block.T.astype(bf16)
    for at, grad in ((0, dk), (1, dv)):
        to_far_ref[at] = grad[0:ROWS].astype(bf16)
        to_near_ref[at] = grad[ROWS : 2 * ROWS].astype(bf16)
        own_ref[at] = grad[2 * ROWS :]


def attention_backward(low, gain, q, u, k, v, near, far):
    f32, bf16 = jnp.float32, jnp.bfloat16
    groups = k.shape[1] // HEAD
    row = pl.BlockSpec((1, ROWS), lambda g: (0, 0))
    wide = pl.BlockSpec((ROWS, PER * HEAD), lambda g: (0, g))
    head = pl.BlockSpec((ROWS, HEAD), lambda g: (0, g))
    pair = pl.BlockSpec((2, ROWS, HEAD), lambda g: (0, 0, g))
    pair_shape = (2, ROWS, groups * HEAD)
    return pl.pallas_call(
        attention_kernel,
        grid=(groups,),
        in_specs=[row, row, wide, wide, head, head, pair, pair],
        out_specs=[wide, pair, pair, pair],
        out_shape=[
            jax.ShapeDtypeStruct(q.shape, bf16),
            jax.ShapeDtypeStruct(pair_shape, f32),
            jax.ShapeDtypeStruct(pair_shape, bf16),
            jax.ShapeDtypeStruct(pair_shape, bf16),
        ],
        scratch_shapes=[
            pltpu.VMEM((2, REACH, HALF), f32),
            pltpu.VMEM((WINDOW, HEAD), bf16),
            pltpu.VMEM((WINDOW, HEAD), bf16),
            pltpu.VMEM((HEAD, WINDOW), bf16),
            pltpu.VMEM((REACH, HEAD), bf16),
            pltpu.VMEM((REACH, HEAD), bf16),
            pltpu.VMEM((REACH, REACH), f32),
            pltpu.VMEM((REACH, REACH), f32),
            pltpu.VMEM((REACH, REACH), bf16),
            pltpu.VMEM((REACH, REACH), bf16),
            pltpu.VMEM((WINDOW, HEAD), f32),
            pltpu.VMEM((WINDOW, HEAD), f32),
        ],
        compiler_params=pltpu.CompilerParams(vmem_limit_bytes=40 * 1024 * 1024),
    )(low, gain, q, u, k, v, near, far)


def local(queries, keys, values, upstream, lengths, group_ids, rewards):
    groups_all = GRP_ROW * lax.axis_size("grp")
    pair = jnp.stack([keys[0], values[0]])
    near = shifted(pair, "ctx", 1)
    far = shifted(pair, "ctx", 2)

    row_lengths = lengths[0]
    row_rewards = rewards[0]
    member = group_ids[0][:, None] == jnp.arange(groups_all, dtype=jnp.int32)[None, :]
    local_sums = jnp.sum(jnp.where(member, row_rewards[:, None], 0.0), axis=0)
    local_counts = jnp.sum(member.astype(jnp.float32), axis=0)
    everyone = lax.all_gather(
        jnp.concatenate([local_sums, local_counts])[None], "grp", tiled=True
    )
    both = jnp.sum(everyone, axis=0)
    own_sum = jnp.sum(jnp.where(member, both[None, :groups_all], 0.0), axis=1)
    own_count = jnp.sum(jnp.where(member, both[None, groups_all:], 0.0), axis=1)
    advantage = row_rewards - (own_sum - row_rewards) / jnp.maximum(own_count - 1.0, 1.0)

    starts = jnp.cumsum(row_lengths) - row_lengths
    first_row = lax.axis_index("ctx") * ROWS
    position = first_row + jnp.arange(ROWS, dtype=jnp.int32)
    begun = starts[None, :] <= position[:, None]
    seg_start = jnp.max(jnp.where(begun, starts[None, :], 0), axis=1)
    picked = begun & (starts[None, :] == seg_start[:, None])
    token_weight = jnp.sum(jnp.where(picked, advantage[None, :], 0.0), axis=1)
    low = seg_start - (first_row - SPAN * ROWS)

    dq, own, to_near, to_far = attention_backward(
        low[None], (token_weight * SCALE)[None], queries[0], upstream[0], keys[0], values[0], near, far
    )
    total = (
        own
        + shifted(to_near, "ctx", -1).astype(jnp.float32)
        + shifted(to_far, "ctx", -2).astype(jnp.float32)
    )
    key_out = (total[0] * (token_weight * SCALE)[:, None]).astype(jnp.bfloat16)
    value_out = (total[1] * token_weight[:, None]).astype(jnp.bfloat16)
    return (dq[None], key_out[None], value_out[None])


def solution(mesh):
    in_specs = (
        P("grp", "ctx", None),
        P("grp", "ctx", None),
        P("grp", "ctx", None),
        P("grp", "ctx", None),
        P("grp", None),
        P("grp", None),
        P("grp", None),
    )
    out_specs = (P("grp", "ctx", None), P("grp", "ctx", None), P("grp", "ctx", None))
    return jax.shard_map(local, mesh=mesh, in_specs=in_specs, out_specs=out_specs, check_vma=False)
```

time: 173 us -> 87.8 us (0.51)
  the two profiles are of different devices: /device:TPU:268 before, /device:TPU:404 now
where the time goes in v1:
time: 87.8 us; the launch traced here: 87.4 us
  waiting for transfers between devices  34.1 us (39%)
  Pallas kernels  15.7 us (18%)
  starting transfers between devices  14.3 us (16%)
  blocking collectives  10.6 us (12%)
  local copies, waits for them, and re-layouts  6.05 us (7%)
  other arithmetic  5.29 us (6%)
  between operations  1.4 us (2%)
    ppermute x4, waiting for transfers between devices, shifted(): return lax.ppermute(x, axis, pairs)  34.1 us
    pallas_call x1, Pallas kernels, attention_backward(): pl.pallas_call(attention_kernel, grid=(groups,), in_specs=[row, row, wide...  15.7 us
    ppermute x4, starting transfers between devices, shifted(): return lax.ppermute(x, axis, pairs)  14.3 us
    unnamed x1, blocking collectives  10.6 us
    unnamed x11, local copies, waits for them, and re-layouts  4.93 us
  transfers between devices with their start and end apart: 4, of which 3 were waited for; matrix products, arithmetic and copies ran while one was open for 6% of the time, Pallas kernels for 0%

profile of v1, /device:TPU:404, one launch (start us, length us, event | category | flops | bytes accessed | tf_op | source)
XLA Modules:
  0.0 87.4 jit_solution(13923738900271957170)
XLA Ops:
  0.6 0.0 copy-start.2
  0.6 0.0 copy-start.3
  0.7 1.0 %constant_dynamic-update-slice_fusion.1 = bf16[2,256,512]{2,1,0:T(8,128)(2,1)S(1)} fusion(bf16[1,256,512]{2,1,0:T(8,128)(2,1)} %param.8), kind=kLoop, calls=%fused_computation.15 | loop fusion | bytes 524288
  1.7 1.0 %constant_dynamic-update-slice_fusion = bf16[2,256,512]{2,1,0:T(8,128)(2,1)S(1)} fusion(bf16[2,256,512]{2,1,0:T(8,128)(2,1)S(1)} %constant_dynamic-update-slice_fusion.1, bf16[1,256,512]{2,1,0:T(8,128)(2,1)} %param.9), kind=kLoop, calls=%fused_computation.14 | loop fusion | bytes 524288 | tf_op jit(solution)/shard_map/stack | solution.py:140
  2.7 2.9 %collective-permute-start.1 = (bf16[2,256,512]{2,1,0:T(8,128)(2,1)S(1)}, bf16[2,256,512]{2,1,0:T(8,128)(2,1)S(1)}, u32[]{:S(2)}, u32[]{:S(2)}) collective-permute-start(bf16[2,256,512]{2,1,0:T(8,128)(2,1)S(1)} %constant_dynamic-update-slice_fusion), channel_id=1, source_target_pairs={{0,16},{8,24},{16,32},{24,40},{32,48},{40,56},{48,64},{56,72},{64,... | collective-permute-start | bytes 1572872 | tf_op jit(solution)/shard_map/ppermute | solution.py:28
  5.5 4.0 %collective-permute-start = (bf16[2,256,512]{2,1,0:T(8,128)(2,1)S(1)}, bf16[2,256,512]{2,1,0:T(8,128)(2,1)S(1)}, u32[]{:S(2)}, u32[]{:S(2)}) collective-permute-start(bf16[2,256,512]{2,1,0:T(8,128)(2,1)S(1)} %constant_dynamic-update-slice_fusion), channel_id=1, source_target_pairs={{0,8},{8,16},{16,24},{24,32},{32,40},{40,48},{48,56},{56,64},{64,7... | collective-permute-start | bytes 1572872 | tf_op jit(solution)/shard_map/ppermute | solution.py:28
  9.6 0.9 %reduce-window_clone.1 = s32[1,64]{1,0:T(1,128)S(1)} reduce-window(s32[1,64]{1,0:T(1,128)} %param.11, s32[]{:T(128)} %constant.6.clone.1), window={size=1x64 pad=0_0x63_0}, to_apply=%region_0.1 | reduce-window | flops 4032 | bytes 516 | tf_op jit(solution)/shard_map/reduce-window.clone
  10.5 0.7 subtract_bitcast_fusion
  11.1 1.3 %dynamic-slice = u32[1]{0:T(128)} dynamic-slice(u32[512]{0:T(512)} %constant.35, u32[]{:T(128)S(6)} %add.30), dynamic_slice_sizes={1} | dynamic-slice | bytes 12
  13.0 0.8 select_reduce_fusion.3
  13.8 0.2 maximum_dynamic-update-slice_fusion
  14.0 10.6 %all-reduce = f32[512]{0:T(512)S(1)} all-reduce(f32[512]{0:T(512)S(1)} %maximum_dynamic-update-slice_fusion), channel_id=2, replica_groups=mesh['ctx'=64,'grp'=8] {'grp'}, use_global_device_ids=true, to_apply=%add | all-reduce | flops 512 | bytes 4096
  24.6 0.1 reshape.70
  24.7 0.1 fusion.5
  24.7 0.1 fusion.2
  24.8 0.7 select_reduce_fusion.2
  25.6 0.7 fusion.4
  26.2 0.1 select_reduce_fusion
  26.4 0.0 collective-permute-done.1.far_ref
  26.4 4.6 %collective-permute-done.near_ref = bf16[2,256,512]{2,1,0:T(8,128)(2,1)S(1)} collective-permute-done((bf16[2,256,512]{2,1,0:T(8,128)(2,1)S(1)}, bf16[2,256,512]{2,1,0:T(8,128)(2,1)S(1)}, u32[]{:S(2)}, u32[]{:S(2)}) %collective-permute-start) | collective-permute-done | bytes 524320 | tf_op jit(solution)/shard_map/ppermute | solution.py:28
  30.9 0.0 copy-done.2
  31.0 0.0 copy-done.3
  31.0 0.0 copy-start
  31.0 1.3 %copy-done = bf16[1,256,2560]{2,1,0:T(8,128)(2,1)S(1)} copy-done((bf16[1,256,2560]{2,1,0:T(8,128)(2,1)S(1)}, bf16[1,256,2560]{2,1,0:T(8,128)(2,1)}, u32[]{:S(2)}) %copy-start) | copy-done | bytes 1310744
  32.3 1.3 %copy-done.1 = bf16[1,256,2560]{2,1,0:T(8,128)(2,1)S(1)} copy-done((bf16[1,256,2560]{2,1,0:T(8,128)(2,1)S(1)}, bf16[1,256,2560]{2,1,0:T(8,128)(2,1)}, u32[]{:S(2)}) %copy-start.1) | copy-done | bytes 1310744
  33.6 15.7 %shard_map.94 = (bf16[256,2560]{1,0:T(8,128)(2,1)}, f32[2,256,512]{2,1,0:T(8,128)S(1)}, bf16[2,256,512]{2,1,0:T(8,128)(2,1)S(1)}, bf16[2,256,512]{2,1,0:T(8,128)(2,1)S(1)}) custom-call(s32[1,256]{1,0:T(1,128)S(1)} %bitcast.31, f32[1,256]{1,0:T(1,128)S(1)} %bitcast.30, bf16[256,2560]{1,0:T(8,128)(2,1)S(1)} %bitcast.26, bf16[256,2560]{1,0:T(8,128)(2,1)S(1)} %bitcast.27, ...), custom_call_target="tpu_custom_call" | custom-call | tf_op jit(solution)/shard_map/pallas_call | solution.py:109
  49.3 2.5 %collective-permute-start.2 = (bf16[2,256,512]{2,1,0:T(8,128)(2,1)S(1)}, bf16[2,256,512]{2,1,0:T(8,128)(2,1)S(1)}, u32[]{:S(2)}, u32[]{:S(2)}) collective-permute-start(bf16[2,256,512]{2,1,0:T(8,128)(2,1)S(1)} %get-tuple-element.9), channel_id=1, source_target_pairs={{8,0},{16,8},{24,16},{32,24},{40,32},{48,40},{56,48},{64,56},{72,6... | collective-permute-start | bytes 1572872 | tf_op jit(solution)/shard_map/ppermute | solution.py:28
  51.8 4.9 %collective-permute-start.3 = (bf16[2,256,512]{2,1,0:T(8,128)(2,1)S(1)}, bf16[2,256,512]{2,1,0:T(8,128)(2,1)S(1)}, u32[]{:S(2)}, u32[]{:S(2)}) collective-permute-start(bf16[2,256,512]{2,1,0:T(8,128)(2,1)S(1)} %get-tuple-element.10), channel_id=1, source_target_pairs={{16,0},{24,8},{32,16},{40,24},{48,32},{56,40},{64,48},{72,56},{80,... | collective-permute-start | bytes 1572872 | tf_op jit(solution)/shard_map/ppermute | solution.py:28
  56.7 9.2 %collective-permute-done.2 = bf16[2,256,512]{2,1,0:T(8,128)(2,1)S(1)} collective-permute-done((bf16[2,256,512]{2,1,0:T(8,128)(2,1)S(1)}, bf16[2,256,512]{2,1,0:T(8,128)(2,1)S(1)}, u32[]{:S(2)}, u32[]{:S(2)}) %collective-permute-start.2) | collective-permute-done | bytes 524320 | tf_op jit(solution)/shard_map/ppermute | solution.py:28
  66.0 20.3 %collective-permute-done.3 = bf16[2,256,512]{2,1,0:T(8,128)(2,1)S(1)} collective-permute-done((bf16[2,256,512]{2,1,0:T(8,128)(2,1)S(1)}, bf16[2,256,512]{2,1,0:T(8,128)(2,1)S(1)}, u32[]{:S(2)}, u32[]{:S(2)}) %collective-permute-start.3) | collective-permute-done | bytes 524320 | tf_op jit(solution)/shard_map/ppermute | solution.py:28
  86.2 0.2 convert_add_fusion
  86.5 0.9 %fusion = (bf16[1,256,512]{2,1,0:T(8,128)(2,1)}, bf16[1,256,512]{2,1,0:T(8,128)(2,1)}) fusion(f32[2,256,512]{2,1,0:T(8,128)S(1)} %convert_add_fusion, f32[256]{0:T(256)S(1)} %select_reduce_fusion, f32[256]{0:T(256)S(1)} %broadcast_multiply_fusion), kind=kLoop, calls=%fused_computation.2 | loop fusion | flops 524288 | bytes 1574912 | tf_op jit(solution)/shard_map/convert_element_type | solution.py:175
  (6 shorter events, 0.0 us)
Async XLA Ops:
  0.6 30.3 %copy-start.2 = (bf16[1,256,512]{2,1,0:T(8,128)(2,1)S(1)}, bf16[1,256,512]{2,1,0:T(8,128)(2,1)}, u32[]{:S(2)}) copy-start(bf16[1,256,512]{2,1,0:T(8,128)(2,1)} %param.8) | copy-start | bytes 786436
  0.6 30.3 %copy-start.3 = (bf16[1,256,512]{2,1,0:T(8,128)(2,1)S(1)}, bf16[1,256,512]{2,1,0:T(8,128)(2,1)}, u32[]{:S(2)}) copy-start(bf16[1,256,512]{2,1,0:T(8,128)(2,1)} %param.9) | copy-start | bytes 786436
  2.7 23.7 %collective-permute-start.1 = (bf16[2,256,512]{2,1,0:T(8,128)(2,1)S(1)}, bf16[2,256,512]{2,1,0:T(8,128)(2,1)S(1)}, u32[]{:S(2)}, u32[]{:S(2)}) collective-permute-start(bf16[2,256,512]{2,1,0:T(8,128)(2,1)S(1)} %constant_dynamic-update-slice_fusion), channel_id=1, source_target_pairs={{0,16},{8,24},{16,32},{24,40},{32,48},{40,56},{48,64},{56,72},{64,... | collective-permute-start | bytes 1572872 | tf_op jit(solution)/shard_map/ppermute | solution.py:28
  5.5 25.4 %collective-permute-start = (bf16[2,256,512]{2,1,0:T(8,128)(2,1)S(1)}, bf16[2,256,512]{2,1,0:T(8,128)(2,1)S(1)}, u32[]{:S(2)}, u32[]{:S(2)}) collective-permute-start(bf16[2,256,512]{2,1,0:T(8,128)(2,1)S(1)} %constant_dynamic-update-slice_fusion), channel_id=1, source_target_pairs={{0,8},{8,16},{16,24},{24,32},{32,40},{40,48},{48,56},{56,64},{64,7... | collective-permute-start | bytes 1572872 | tf_op jit(solution)/shard_map/ppermute | solution.py:28
  31.0 1.3 %copy-start = (bf16[1,256,2560]{2,1,0:T(8,128)(2,1)S(1)}, bf16[1,256,2560]{2,1,0:T(8,128)(2,1)}, u32[]{:S(2)}) copy-start(bf16[1,256,2560]{2,1,0:T(8,128)(2,1)} %param.7) | copy-start | bytes 3932164
  32.3 1.3 %copy-start.1 = (bf16[1,256,2560]{2,1,0:T(8,128)(2,1)S(1)}, bf16[1,256,2560]{2,1,0:T(8,128)(2,1)}, u32[]{:S(2)}) copy-start(bf16[1,256,2560]{2,1,0:T(8,128)(2,1)} %param.10) | copy-start | bytes 3932164
  49.3 16.7 %collective-permute-start.2 = (bf16[2,256,512]{2,1,0:T(8,128)(2,1)S(1)}, bf16[2,256,512]{2,1,0:T(8,128)(2,1)S(1)}, u32[]{:S(2)}, u32[]{:S(2)}) collective-permute-start(bf16[2,256,512]{2,1,0:T(8,128)(2,1)S(1)} %get-tuple-element.9), channel_id=1, source_target_pairs={{8,0},{16,8},{24,16},{32,24},{40,32},{48,40},{56,48},{64,56},{72,6... | collective-permute-start | bytes 1572872 | tf_op jit(solution)/shard_map/ppermute | solution.py:28
  51.8 34.4 %collective-permute-start.3 = (bf16[2,256,512]{2,1,0:T(8,128)(2,1)S(1)}, bf16[2,256,512]{2,1,0:T(8,128)(2,1)S(1)}, u32[]{:S(2)}, u32[]{:S(2)}) collective-permute-start(bf16[2,256,512]{2,1,0:T(8,128)(2,1)S(1)} %get-tuple-element.10), channel_id=1, source_target_pairs={{16,0},{24,8},{32,16},{40,24},{48,32},{56,40},{64,48},{72,56},{80,... | collective-permute-start | bytes 1572872 | tf_op jit(solution)/shard_map/ppermute | solution.py:28

commit v2 on v1

--- a/solution.py
+++ b/solution.py
@@ -20,6 +20,9 @@
 SCALE = 1.0 / math.sqrt(HEAD)
 EXP_SCALE = SCALE * math.log2(math.e)
 EXCLUDED = -1e30
+PARTS = 2
+VMEM_BYTES = 32 * 1024 * 1024
+COST_FLOPS = 4_000_000_000
 
 
 def shifted(x, axis, by):
@@ -28,11 +31,10 @@
     return lax.ppermute(x, axis, pairs)
 
 
-def attention_kernel(
-    low_ref, gain_ref, q_ref, u_ref, k_ref, v_ref, near_ref, far_ref,
-    dq_ref, own_ref, to_near_ref, to_far_ref,
-    mask, kw, vw, kt, qj, uj, s, uv, p, ds, dk, dv,
-):
+def attention_kernel(*refs):
+    low_ref, q_ref, u_ref, k_ref, v_ref, near_ref, far_ref = refs[-23:-16]
+    dq_ref, own_ref, to_near_ref, to_far_ref = refs[-16:-12]
+    mask, kw, vw, kt, qj, uj, s, uv, p, ds, dk, dv = refs[-12:]
     f32, bf16 = jnp.float32, jnp.bfloat16
 
     @pl.when(pl.program_id(0) == 0)
@@ -88,9 +90,8 @@
         dv[keys] += jnp.dot(p[...], uj[...], preferred_element_type=f32)
         dk[keys] += jnp.dot(ds[...], qj[...], preferred_element_type=f32)
         dq_t = jnp.dot(kt[:, keys], ds[...], preferred_element_type=f32)
-        gain = gain_ref[:, rows]
         for h in range(PER):
-            block = dq_t[:, h * HALF : (h + 1) * HALF] * gain
+            block = dq_t[:, h * HALF : (h + 1) * HALF]
             dq_ref[rows, h * HEAD : (h + 1) * HEAD] = block.T.astype(bf16)
     for at, grad in ((0, dk), (1, dv)):
         to_far_ref[at] = grad[0:ROWS].astype(bf16)
@@ -98,18 +99,20 @@
         own_ref[at] = grad[2 * ROWS :]
 
 
-def attention_backward(low, gain, q, u, k, v, near, far):
+def attention_backward(part, low, q, u, k, v, near, far, before):
     f32, bf16 = jnp.float32, jnp.bfloat16
-    groups = k.shape[1] // HEAD
+    groups = far.shape[2] // HEAD
+    first = part * groups
     row = pl.BlockSpec((1, ROWS), lambda g: (0, 0))
-    wide = pl.BlockSpec((ROWS, PER * HEAD), lambda g: (0, g))
-    head = pl.BlockSpec((ROWS, HEAD), lambda g: (0, g))
+    wide = pl.BlockSpec((ROWS, PER * HEAD), lambda g: (0, first + g))
+    head = pl.BlockSpec((ROWS, HEAD), lambda g: (0, first + g))
     pair = pl.BlockSpec((2, ROWS, HEAD), lambda g: (0, 0, g))
     pair_shape = (2, ROWS, groups * HEAD)
     return pl.pallas_call(
         attention_kernel,
         grid=(groups,),
-        in_specs=[row, row, wide, wide, head, head, pair, pair],
+        in_specs=[pl.BlockSpec(memory_space=pl.ANY)] * len(before)
+        + [row, wide, wide, head, head, pair, pair],
         out_specs=[wide, pair, pair, pair],
         out_shape=[
             jax.ShapeDtypeStruct(q.shape, bf16),
@@ -131,49 +134,81 @@
             pltpu.VMEM((WINDOW, HEAD), f32),
             pltpu.VMEM((WINDOW, HEAD), f32),
         ],
-        compiler_params=pltpu.CompilerParams(vmem_limit_bytes=40 * 1024 * 1024),
-    )(low, gain, q, u, k, v, near, far)
-
-
-def local(queries, keys, values, upstream, lengths, group_ids, rewards):
+        input_output_aliases={0: 0} if before else {},
+        compiler_params=pltpu.CompilerParams(vmem_limit_bytes=VMEM_BYTES),
+        cost_estimate=pl.CostEstimate(
+            flops=COST_FLOPS * groups,
+            bytes_accessed=4 * 1024 * 1024,
+            transcendentals=groups * 2 * REACH * REACH,
+        ),
+    )(*before, low, q, u, k, v, near, far)
+
+
+def after_kernel(x_ref, *refs):
+    refs[-1][...] = x_ref[...]
+
+
+def after(x, *others):
+    return pl.pallas_call(
+        after_kernel,
+        in_specs=[pl.BlockSpec(memory_space=pltpu.VMEM)] + [pl.BlockSpec(memory_space=pl.ANY)] * len(others),
+        out_specs=pl.BlockSpec(memory_space=pltpu.VMEM),
+        out_shape=jax.ShapeDtypeStruct(x.shape, x.dtype),
+    )(x, *others)
+
+
+def group_stats(group_ids, rewards):
     groups_all = GRP_ROW * lax.axis_size("grp")
-    pair = jnp.stack([keys[0], values[0]])
-    near = shifted(pair, "ctx", 1)
-    far = shifted(pair, "ctx", 2)
-
-    row_lengths = lengths[0]
-    row_rewards = rewards[0]
-    member = group_ids[0][:, None] == jnp.arange(groups_all, dtype=jnp.int32)[None, :]
-    local_sums = jnp.sum(jnp.where(member, row_rewards[:, None], 0.0), axis=0)
-    local_counts = jnp.sum(member.astype(jnp.float32), axis=0)
-    everyone = lax.all_gather(
-        jnp.concatenate([local_sums, local_counts])[None], "grp", tiled=True
+    member = group_ids[:, None] == jnp.arange(groups_all, dtype=jnp.int32)[None, :]
+    sums = jnp.sum(jnp.where(member, rewards[:, None], 0.0), axis=0)
+    counts = jnp.sum(member.astype(jnp.float32), axis=0)
+    return member, jnp.concatenate([sums, counts])[None]
+
+
+def advantage_of(member, stats, rewards):
+    rows, groups_all = lax.axis_size("grp"), member.shape[1]
+    everyone = lax.all_to_all(
+        jnp.broadcast_to(stats, (rows, stats.shape[1])), "grp", 0, 0, tiled=True
     )
     both = jnp.sum(everyone, axis=0)
     own_sum = jnp.sum(jnp.where(member, both[None, :groups_all], 0.0), axis=1)
     own_count = jnp.sum(jnp.where(member, both[None, groups_all:], 0.0), axis=1)
-    advantage = row_rewards - (own_sum - row_rewards) / jnp.maximum(own_count - 1.0, 1.0)
-
-    starts = jnp.cumsum(row_lengths) - row_lengths
+    return rewards - (own_sum - rewards) / jnp.maximum(own_count - 1.0, 1.0)
+
+
+def local(queries, keys, values, upstream, lengths, group_ids, rewards):
+    width = keys.shape[2] // PARTS
+    halos = []
+    for part in range(PARTS):
+        cols = slice(part * width, (part + 1) * width)
+        pair = jnp.stack([keys[0, :, cols], values[0, :, cols]])
+        halos.append((shifted(pair, "ctx", 1), shifted(pair, "ctx", 2)))
+
+    starts = jnp.cumsum(lengths[0]) - lengths[0]
     first_row = lax.axis_index("ctx") * ROWS
     position = first_row + jnp.arange(ROWS, dtype=jnp.int32)
     begun = starts[None, :] <= position[:, None]
     seg_start = jnp.max(jnp.where(begun, starts[None, :], 0), axis=1)
+    low = (seg_start - (first_row - SPAN * ROWS))[None]
+
+    before, received = [], []
+    for part, (near, far) in enumerate(halos):
+        dq, own, to_near, to_far = attention_backward(
+            part, low, queries[0], upstream[0], keys[0], values[0], near, far, before
+        )
+        before = [dq]
+        received.append((own, shifted(to_near, "ctx", -1), shifted(to_far, "ctx", -2)))
+
+    member, stats = group_stats(group_ids[0], rewards[0])
+    advantage = advantage_of(member, after(stats, *received[0][1:]), rewards[0])
     picked = begun & (starts[None, :] == seg_start[:, None])
-    token_weight = jnp.sum(jnp.where(picked, advantage[None, :], 0.0), axis=1)
-    low = seg_start - (first_row - SPAN * ROWS)
-
-    dq, own, to_near, to_far = attention_backward(
-        low[None], (token_weight * SCALE)[None], queries[0], upstream[0], keys[0], values[0], near, far
-    )
-    total = (
-        own
-        + shifted(to_near, "ctx", -1).astype(jnp.float32)
-        + shifted(to_far, "ctx", -2).astype(jnp.float32)
-    )
-    key_out = (total[0] * (token_weight * SCALE)[:, None]).astype(jnp.bfloat16)
-    value_out = (total[1] * token_weight[:, None]).astype(jnp.bfloat16)
-    return (dq[None], key_out[None], value_out[None])
+    weight = jnp.sum(jnp.where(picked, advantage[None, :], 0.0), axis=1)[:, None]
+    scaled = weight * SCALE
+    dq = (dq.astype(jnp.float32) * scaled).astype(jnp.bfloat16)
+    totals = [own + a.astype(jnp.float32) + b.astype(jnp.float32) for own, a, b in received]
+    dk = [(t[0] * scaled).astype(jnp.bfloat16) for t in totals]
+    dv = [(t[1] * weight).astype(jnp.bfloat16) for t in totals]
+    return (dq[None], jnp.concatenate(dk, axis=1)[None], jnp.concatenate(dv, axis=1)[None])
 
 
 def solution(mesh):

time: 87.8 us -> 74.8 us (0.85)
  the two profiles are of different devices: /device:TPU:404 before, /device:TPU:388 now
where the time goes in v2:
time: 74.8 us; the launch traced here: 74.4 us
  starting transfers between devices  35.7 us (48%)
  Pallas kernels  16.9 us (23%)
  waiting for transfers between devices  8.86 us (12%)
  other arithmetic  6.1 us (8%)
  local copies, waits for them, and re-layouts  5.9 us (8%)
  between operations  0.87 us (1%)
    ppermute x8, starting transfers between devices, shifted(): return lax.ppermute(x, axis, pairs)  31.2 us
    pallas_call x2, Pallas kernels, attention_backward(): pl.pallas_call(attention_kernel, grid=(groups,), in_specs=[pl.BlockSpec(m...  15.8 us
    ppermute x8, waiting for transfers between devices, shifted(): return lax.ppermute(x, axis, pairs)  4.8 us
    all_to_all x1, starting transfers between devices, advantage_of(): lax.all_to_all(jnp.broadcast_to(stats, (rows, stats.shape[1])), 'grp', 0,...  4.47 us
    all_to_all x1, waiting for transfers between devices, advantage_of(): lax.all_to_all(jnp.broadcast_to(stats, (rows, stats.shape[1])), 'grp', 0,...  4.06 us
    unnamed x16, local copies, waits for them, and re-layouts  3.35 us
  transfers between devices with their start and end apart: 9, of which 2 were waited for; matrix products, arithmetic and copies ran while one was open for 6% of the time, Pallas kernels for 23%

profile of v2, /device:TPU:388, one launch (start us, length us, event | category | flops | bytes accessed | tf_op | source)
XLA Modules:
  0.0 74.4 jit_solution(11770496745125931644)
XLA Ops:
  0.7 1.2 %fusion.12 = (bf16[1,256,256]{2,1,0:T(8,128)(2,1)S(1)}, bf16[1,256,256]{2,1,0:T(8,128)(2,1)S(1)}, bf16[1,256,256]{2,1,0:T(8,128)(2,1)S(1)}, bf16[1,256,256]{2,1,0:T(8,128)(2,1)S(1)}) fusion(bf16[1,256,512]{2,1,0:T(8,128)(2,1)} %param.8, bf16[1,256,512]{2,1,0:T(8,128)(2,1)} %param.9), kind=kLoop, calls=%fused_computation.38 | loop fusion | bytes 1048576 | tf_op jit(solution)/shard_map/slice | solution.py:184
  1.9 2.9 %collective-permute-start.1 = (bf16[2,256,256]{2,1,0:T(8,128)(2,1)S(1)}, bf16[2,256,256]{2,1,0:T(8,128)(2,1)S(1)}, u32[]{:S(2)}, u32[]{:S(2)}) collective-permute-start(bf16[2,256,256]{2,1,0:T(8,128)(2,1)S(1)} %pad_maximum_fusion), channel_id=1, source_target_pairs={{0,16},{8,24},{16,32},{24,40},{32,48},{40,56},{48,64},{56,72},{64,... | collective-permute-start | bytes 786440 | tf_op jit(solution)/shard_map/ppermute | solution.py:31
  4.8 4.0 %collective-permute-start = (bf16[2,256,256]{2,1,0:T(8,128)(2,1)S(1)}, bf16[2,256,256]{2,1,0:T(8,128)(2,1)S(1)}, u32[]{:S(2)}, u32[]{:S(2)}) collective-permute-start(bf16[2,256,256]{2,1,0:T(8,128)(2,1)S(1)} %pad_maximum_fusion), channel_id=1, source_target_pairs={{0,8},{8,16},{16,24},{24,32},{32,40},{40,48},{48,56},{56,64},{64,7... | collective-permute-start | bytes 786440 | tf_op jit(solution)/shard_map/ppermute | solution.py:31
  8.8 0.7 pad_maximum_fusion.1
  9.5 3.4 %collective-permute-start.3 = (bf16[2,256,256]{2,1,0:T(8,128)(2,1)}, bf16[2,256,256]{2,1,0:T(8,128)(2,1)S(1)}, u32[]{:S(2)}, u32[]{:S(2)}) collective-permute-start(bf16[2,256,256]{2,1,0:T(8,128)(2,1)} %pad_maximum_fusion.1), channel_id=1, source_target_pairs={{0,16},{8,24},{16,32},{24,40},{32,48},{40,56},{48,64},{56,72},{64,... | collective-permute-start | bytes 786440 | tf_op jit(solution)/shard_map/ppermute | solution.py:31
  13.0 2.8 %collective-permute-start.2 = (bf16[2,256,256]{2,1,0:T(8,128)(2,1)}, bf16[2,256,256]{2,1,0:T(8,128)(2,1)S(1)}, u32[]{:S(2)}, u32[]{:S(2)}) collective-permute-start(bf16[2,256,256]{2,1,0:T(8,128)(2,1)} %pad_maximum_fusion.1), channel_id=1, source_target_pairs={{0,8},{8,16},{16,24},{24,32},{32,40},{40,48},{48,56},{56,64},{64,7... | collective-permute-start | bytes 786440 | tf_op jit(solution)/shard_map/ppermute | solution.py:31
  15.8 0.2 reduce-window_clone.1
  16.1 0.1 fusion.9
  16.2 0.1 select_reduce_fusion.3
  16.3 0.6 maximum_bitcast_fusion.2.x_ref
  16.9 4.8 %collective-permute-done.refs_5_ = bf16[2,256,256]{2,1,0:T(8,128)(2,1)S(1)} collective-permute-done((bf16[2,256,256]{2,1,0:T(8,128)(2,1)S(1)}, bf16[2,256,256]{2,1,0:T(8,128)(2,1)S(1)}, u32[]{:S(2)}, u32[]{:S(2)}) %collective-permute-start) | collective-permute-done | bytes 262176 | tf_op jit(solution)/shard_map/ppermute | solution.py:31
  21.7 1.3 %copy-done.2 = bf16[1,256,2560]{2,1,0:T(8,128)(2,1)S(1)} copy-done((bf16[1,256,2560]{2,1,0:T(8,128)(2,1)S(1)}, bf16[1,256,2560]{2,1,0:T(8,128)(2,1)}, u32[]{:S(2)}) %copy-start.2) | copy-done | bytes 1310744
  23.0 1.3 %copy-done.3 = bf16[1,256,2560]{2,1,0:T(8,128)(2,1)S(1)} copy-done((bf16[1,256,2560]{2,1,0:T(8,128)(2,1)S(1)}, bf16[1,256,2560]{2,1,0:T(8,128)(2,1)}, u32[]{:S(2)}) %copy-start.3) | copy-done | bytes 1310744
  24.3 7.6 %shard_map.94 = (bf16[256,2560]{1,0:T(8,128)(2,1)S(1)}, f32[2,256,256]{2,1,0:T(8,128)S(1)}, bf16[2,256,256]{2,1,0:T(8,128)(2,1)S(1)}, bf16[2,256,256]{2,1,0:T(8,128)(2,1)S(1)}) custom-call(s32[1,256]{1,0:T(1,128)S(1)} %bitcast.61, bf16[256,2560]{1,0:T(8,128)(2,1)S(1)} %bitcast.63, bf16[256,2560]{1,0:T(8,128)(2,1)S(1)} %bitcast.65, ...), custom_call_target="tpu_custom_call" | custom-call | flops 8000000000 | bytes 4194304 | tf_op jit(solution)/shard_map/pallas_call | solution.py:111
  31.9 1.9 %collective-permute-start.4 = (bf16[2,256,256]{2,1,0:T(8,128)(2,1)S(1)}, bf16[2,256,256]{2,1,0:T(8,128)(2,1)S(1)}, u32[]{:S(2)}, u32[]{:S(2)}) collective-permute-start(bf16[2,256,256]{2,1,0:T(8,128)(2,1)S(1)} %get-tuple-element.13), channel_id=1, source_target_pairs={{8,0},{16,8},{24,16},{32,24},{40,32},{48,40},{56,48},{64,56},{72,6... | collective-permute-start | bytes 786440 | tf_op jit(solution)/shard_map/ppermute | solution.py:31
  33.8 8.0 %collective-permute-start.5 = (bf16[2,256,256]{2,1,0:T(8,128)(2,1)S(1)}, bf16[2,256,256]{2,1,0:T(8,128)(2,1)}, u32[]{:S(2)}, u32[]{:S(2)}) collective-permute-start(bf16[2,256,256]{2,1,0:T(8,128)(2,1)S(1)} %get-tuple-element.14), channel_id=1, source_target_pairs={{16,0},{24,8},{32,16},{40,24},{48,32},{56,40},{64,48},{72,56},{80,... | collective-permute-start | bytes 786440 | tf_op jit(solution)/shard_map/ppermute | solution.py:31
  41.9 8.2 %shard_map.95 = (bf16[256,2560]{1,0:T(8,128)(2,1)S(1)}, f32[2,256,256]{2,1,0:T(8,128)S(1)}, bf16[2,256,256]{2,1,0:T(8,128)(2,1)}, bf16[2,256,256]{2,1,0:T(8,128)(2,1)}) custom-call(bf16[256,2560]{1,0:T(8,128)(2,1)S(1)} %get-tuple-element.11.refs_0_, s32[1,256]{1,0:T(1,128)S(1)} %bitcast.62, ...), custom_call_target="tpu_custom_call", output_to_operand_aliasing={{0}: (0, {})} | custom-call | flops 8000000000 | bytes 4194304 | tf_op jit(solution)/shard_map/pallas_call | solution.py:111
  50.1 1.9 %collective-permute-start.6 = (bf16[2,256,256]{2,1,0:T(8,128)(2,1)}, bf16[2,256,256]{2,1,0:T(8,128)(2,1)S(1)}, u32[]{:S(2)}, u32[]{:S(2)}) collective-permute-start(bf16[2,256,256]{2,1,0:T(8,128)(2,1)} %get-tuple-element.17), channel_id=1, source_target_pairs={{8,0},{16,8},{24,16},{32,24},{40,32},{48,40},{56,48},{64,56},{72,6... | collective-permute-start | bytes 786440 | tf_op jit(solution)/shard_map/ppermute | solution.py:31
  52.0 6.2 %collective-permute-start.7 = (bf16[2,256,256]{2,1,0:T(8,128)(2,1)}, bf16[2,256,256]{2,1,0:T(8,128)(2,1)S(1)}, u32[]{:S(2)}, u32[]{:S(2)}) collective-permute-start(bf16[2,256,256]{2,1,0:T(8,128)(2,1)} %get-tuple-element.18), channel_id=1, source_target_pairs={{16,0},{24,8},{32,16},{40,24},{48,32},{56,40},{64,48},{72,56},{80,... | collective-permute-start | bytes 786440 | tf_op jit(solution)/shard_map/ppermute | solution.py:31
  58.3 0.7 copy-done.4
  59.0 1.2 %shard_map.96 = f32[1,64]{1,0:T(1,128)} custom-call(f32[1,64]{1,0:T(1,128)} %maximum_bitcast_fusion.2.x_ref, bf16[2,256,256]{2,1,0:T(8,128)(2,1)} %copy-done.4, bf16[2,256,256]{2,1,0:T(8,128)(2,1)} %collective-permute-done.5.refs_1_), custom_call_target="tpu_custom_call" | custom-call | tf_op jit(solution)/shard_map/pallas_call | solution.py:152
  60.1 1.3 %broadcast_in_dim.87 = f32[8,1,64]{2,1,0:T(1,128)} broadcast(f32[64]{0:T(128)} %bitcast.71), dimensions={2} | broadcast | bytes 2304 | tf_op jit(solution)/shard_map/broadcast_in_dim | solution.py:171
  61.4 4.5 %all-to-all-start = ((f32[8,1,64]{2,1,0:T(1,128)}), f32[8,1,64]{2,1,0:T(1,128)S(1)}, u32[]{:S(2)}, u32[]{:S(2)}) async-start(f32[8,1,64]{2,1,0:T(1,128)} %broadcast_in_dim.87), calls=%async_computation | async-start | bytes 8192 | tf_op jit(solution)/shard_map/all_to_all | solution.py:170
  65.9 1.1 %convert_add_fusion.1 = f32[2,256,256]{2,1,0:T(8,128)S(1)} fusion(bf16[2,256,256]{2,1,0:T(8,128)(2,1)} %collective-permute-done.5.refs_1_, f32[2,256,256]{2,1,0:T(8,128)S(1)} %get-tuple-element.15, bf16[2,256,256]{2,1,0:T(8,128)(2,1)} %copy-done.4), kind=kLoop, calls=%fused_computation.3 | loop fusion | flops 524288 | bytes 1572864 | tf_op jit(solution)/shard_map/add | solution.py:208
  67.1 4.1 %all-to-all-done = f32[8,1,64]{2,1,0:T(1,128)S(1)} async-done(((f32[8,1,64]{2,1,0:T(1,128)}), f32[8,1,64]{2,1,0:T(1,128)S(1)}, u32[]{:S(2)}, u32[]{:S(2)}) %all-to-all-start) | async-done | bytes 2080 | tf_op jit(solution)/shard_map/all_to_all | solution.py:170
  71.1 0.1 fusion.14
  71.2 0.1 select_reduce_fusion.2
  71.3 0.1 select_reduce_fusion
  71.4 1.3 %fusion = bf16[1,256,2560]{2,1,0:T(8,128)(2,1)} fusion(bf16[256,2560]{1,0:T(8,128)(2,1)S(1)} %get-tuple-element.12, f32[256]{0:T(256)S(1)} %broadcast_multiply_fusion), kind=kLoop, calls=%fused_computation.1 | loop fusion | flops 1966080 | bytes 2622464 | tf_op jit(solution)/shard_map/broadcast_in_dim | solution.py:211
  72.8 0.1 fusion.2
  72.9 0.7 maximum_bitcast_fusion.1
  73.6 0.7 maximum_bitcast_fusion
  (28 shorter events, 0.2 us)
Async XLA Ops:
  0.6 21.0 %copy-start.1 = (bf16[1,256,512]{2,1,0:T(8,128)(2,1)S(1)}, bf16[1,256,512]{2,1,0:T(8,128)(2,1)}, u32[]{:S(2)}) copy-start(bf16[1,256,512]{2,1,0:T(8,128)(2,1)} %param.9) | copy-start | bytes 786436
  0.6 21.0 %copy-start = (bf16[1,256,512]{2,1,0:T(8,128)(2,1)S(1)}, bf16[1,256,512]{2,1,0:T(8,128)(2,1)}, u32[]{:S(2)}) copy-start(bf16[1,256,512]{2,1,0:T(8,128)(2,1)} %param.8) | copy-start | bytes 786436
  0.7 15.2 %copy-start.7 = (s32[1,64]{1,0:T(1,128)S(1)}, s32[1,64]{1,0:T(1,128)}, u32[]{:S(2)}) copy-start(s32[1,64]{1,0:T(1,128)} %param.11) | copy-start | bytes 772
  0.7 15.5 %copy-start.6 = (f32[1,64]{1,0:T(1,128)S(1)}, f32[1,64]{1,0:T(1,128)}, u32[]{:S(2)}) copy-start(f32[1,64]{1,0:T(1,128)} %param.13) | copy-start | bytes 772
  0.7 15.5 %copy-start.5 = (s32[1,64]{1,0:T(1,128)S(1)}, s32[1,64]{1,0:T(1,128)}, u32[]{:S(2)}) copy-start(s32[1,64]{1,0:T(1,128)} %param.12) | copy-start | bytes 772
  1.9 15.0 %collective-permute-start.1 = (bf16[2,256,256]{2,1,0:T(8,128)(2,1)S(1)}, bf16[2,256,256]{2,1,0:T(8,128)(2,1)S(1)}, u32[]{:S(2)}, u32[]{:S(2)}) collective-permute-start(bf16[2,256,256]{2,1,0:T(8,128)(2,1)S(1)} %pad_maximum_fusion), channel_id=1, source_target_pairs={{0,16},{8,24},{16,32},{24,40},{32,48},{40,56},{48,64},{56,72},{64,... | collective-permute-start | bytes 786440 | tf_op jit(solution)/shard_map/ppermute | solution.py:31
  4.8 16.9 %collective-permute-start = (bf16[2,256,256]{2,1,0:T(8,128)(2,1)S(1)}, bf16[2,256,256]{2,1,0:T(8,128)(2,1)S(1)}, u32[]{:S(2)}, u32[]{:S(2)}) collective-permute-start(bf16[2,256,256]{2,1,0:T(8,128)(2,1)S(1)} %pad_maximum_fusion), channel_id=1, source_target_pairs={{0,8},{8,16},{16,24},{24,32},{32,40},{40,48},{48,56},{56,64},{64,7... | collective-permute-start | bytes 786440 | tf_op jit(solution)/shard_map/ppermute | solution.py:31
  9.5 32.3 %collective-permute-start.3 = (bf16[2,256,256]{2,1,0:T(8,128)(2,1)}, bf16[2,256,256]{2,1,0:T(8,128)(2,1)S(1)}, u32[]{:S(2)}, u32[]{:S(2)}) collective-permute-start(bf16[2,256,256]{2,1,0:T(8,128)(2,1)} %pad_maximum_fusion.1), channel_id=1, source_target_pairs={{0,16},{8,24},{16,32},{24,40},{32,48},{40,56},{48,64},{56,72},{64,... | collective-permute-start | bytes 786440 | tf_op jit(solution)/shard_map/ppermute | solution.py:31
  13.0 28.9 %collective-permute-start.2 = (bf16[2,256,256]{2,1,0:T(8,128)(2,1)}, bf16[2,256,256]{2,1,0:T(8,128)(2,1)S(1)}, u32[]{:S(2)}, u32[]{:S(2)}) collective-permute-start(bf16[2,256,256]{2,1,0:T(8,128)(2,1)} %pad_maximum_fusion.1), channel_id=1, source_target_pairs={{0,8},{8,16},{16,24},{24,32},{32,40},{40,48},{48,56},{56,64},{64,7... | collective-permute-start | bytes 786440 | tf_op jit(solution)/shard_map/ppermute | solution.py:31
  21.7 1.3 %copy-start.2 = (bf16[1,256,2560]{2,1,0:T(8,128)(2,1)S(1)}, bf16[1,256,2560]{2,1,0:T(8,128)(2,1)}, u32[]{:S(2)}) copy-start(bf16[1,256,2560]{2,1,0:T(8,128)(2,1)} %param.7) | copy-start | bytes 3932164
  23.0 1.3 %copy-start.3 = (bf16[1,256,2560]{2,1,0:T(8,128)(2,1)S(1)}, bf16[1,256,2560]{2,1,0:T(8,128)(2,1)}, u32[]{:S(2)}) copy-start(bf16[1,256,2560]{2,1,0:T(8,128)(2,1)} %param.10) | copy-start | bytes 3932164
  31.9 26.4 %collective-permute-start.4 = (bf16[2,256,256]{2,1,0:T(8,128)(2,1)S(1)}, bf16[2,256,256]{2,1,0:T(8,128)(2,1)S(1)}, u32[]{:S(2)}, u32[]{:S(2)}) collective-permute-start(bf16[2,256,256]{2,1,0:T(8,128)(2,1)S(1)} %get-tuple-element.13), channel_id=1, source_target_pairs={{8,0},{16,8},{24,16},{32,24},{40,32},{48,40},{56,48},{64,56},{72,6... | collective-permute-start | bytes 786440 | tf_op jit(solution)/shard_map/ppermute | solution.py:31
  33.8 25.2 %collective-permute-start.5 = (bf16[2,256,256]{2,1,0:T(8,128)(2,1)S(1)}, bf16[2,256,256]{2,1,0:T(8,128)(2,1)}, u32[]{:S(2)}, u32[]{:S(2)}) collective-permute-start(bf16[2,256,256]{2,1,0:T(8,128)(2,1)S(1)} %get-tuple-element.14), channel_id=1, source_target_pairs={{16,0},{24,8},{32,16},{40,24},{48,32},{56,40},{64,48},{72,56},{80,... | collective-permute-start | bytes 786440 | tf_op jit(solution)/shard_map/ppermute | solution.py:31
  50.1 16.9 %collective-permute-start.6 = (bf16[2,256,256]{2,1,0:T(8,128)(2,1)}, bf16[2,256,256]{2,1,0:T(8,128)(2,1)S(1)}, u32[]{:S(2)}, u32[]{:S(2)}) collective-permute-start(bf16[2,256,256]{2,1,0:T(8,128)(2,1)} %get-tuple-element.17), channel_id=1, source_target_pairs={{8,0},{16,8},{24,16},{32,24},{40,32},{48,40},{56,48},{64,56},{72,6... | collective-permute-start | bytes 786440 | tf_op jit(solution)/shard_map/ppermute | solution.py:31
  52.0 15.0 %collective-permute-start.7 = (bf16[2,256,256]{2,1,0:T(8,128)(2,1)}, bf16[2,256,256]{2,1,0:T(8,128)(2,1)S(1)}, u32[]{:S(2)}, u32[]{:S(2)}) collective-permute-start(bf16[2,256,256]{2,1,0:T(8,128)(2,1)} %get-tuple-element.18), channel_id=1, source_target_pairs={{16,0},{24,8},{32,16},{40,24},{48,32},{56,40},{64,48},{72,56},{80,... | collective-permute-start | bytes 786440 | tf_op jit(solution)/shard_map/ppermute | solution.py:31
  58.3 0.7 copy-start.4
  61.4 9.7 %all-to-all-start = ((f32[8,1,64]{2,1,0:T(1,128)}), f32[8,1,64]{2,1,0:T(1,128)S(1)}, u32[]{:S(2)}, u32[]{:S(2)}) async-start(f32[8,1,64]{2,1,0:T(1,128)} %broadcast_in_dim.87), calls=%async_computation | async-start | bytes 8192 | tf_op jit(solution)/shard_map/all_to_all | solution.py:170

commit v3 on v2

--- a/solution.py
+++ b/solution.py
@@ -32,7 +32,7 @@
 
 
 def attention_kernel(*refs):
-    low_ref, q_ref, u_ref, k_ref, v_ref, near_ref, far_ref = refs[-23:-16]
+    far_ref, near_ref, low_ref, q_ref, u_ref, k_ref, v_ref = refs[-23:-16]
     dq_ref, own_ref, to_near_ref, to_far_ref = refs[-16:-12]
     mask, kw, vw, kt, qj, uj, s, uv, p, ds, dk, dv = refs[-12:]
     f32, bf16 = jnp.float32, jnp.bfloat16
@@ -102,6 +102,7 @@
 def attention_backward(part, low, q, u, k, v, near, far, before):
     f32, bf16 = jnp.float32, jnp.bfloat16
     groups = far.shape[2] // HEAD
+    q, u = (pltpu.with_memory_space_constraint(x, pltpu.HBM) for x in (q, u))
     first = part * groups
     row = pl.BlockSpec((1, ROWS), lambda g: (0, 0))
     wide = pl.BlockSpec((ROWS, PER * HEAD), lambda g: (0, first + g))
@@ -112,7 +113,7 @@
         attention_kernel,
         grid=(groups,),
         in_specs=[pl.BlockSpec(memory_space=pl.ANY)] * len(before)
-        + [row, wide, wide, head, head, pair, pair],
+        + [pair, pair, row, wide, wide, head, head],
         out_specs=[wide, pair, pair, pair],
         out_shape=[
             jax.ShapeDtypeStruct(q.shape, bf16),
@@ -141,38 +142,42 @@
             bytes_accessed=4 * 1024 * 1024,
             transcendentals=groups * 2 * REACH * REACH,
         ),
-    )(*before, low, q, u, k, v, near, far)
-
-
-def after_kernel(x_ref, *refs):
-    refs[-1][...] = x_ref[...]
-
-
-def after(x, *others):
+    )(*before, far, near, low, q, u, k, v)
+
+
+def stats_kernel(ids_ref, rewards_ref, _, out_ref):
+    copies, groups_all = out_ref.shape[0], out_ref.shape[2] // 2
+    ids = jnp.broadcast_to(ids_ref[...], (groups_all, ids_ref.shape[1]))
+    member = (ids == lax.broadcasted_iota(jnp.int32, ids.shape, 0)).astype(jnp.float32)
+    rewards = jnp.broadcast_to(rewards_ref[...], (copies, ids.shape[1]))
+    sums, counts = (
+        lax.dot_general(
+            x, member, (((1,), (1,)), ((), ())),
+            precision=lax.Precision.HIGHEST, preferred_element_type=jnp.float32,
+        )
+        for x in (rewards, jnp.ones_like(rewards))
+    )
+    stats = jnp.concatenate([sums, counts], axis=1)
+    for i in range(copies):
+        out_ref[i] = stats[i : i + 1]
+
+
+def stats_after(group_ids, rewards, copies, other):
+    vmem = pl.BlockSpec(memory_space=pltpu.VMEM)
     return pl.pallas_call(
-        after_kernel,
-        in_specs=[pl.BlockSpec(memory_space=pltpu.VMEM)] + [pl.BlockSpec(memory_space=pl.ANY)] * len(others),
-        out_specs=pl.BlockSpec(memory_space=pltpu.VMEM),
-        out_shape=jax.ShapeDtypeStruct(x.shape, x.dtype),
-    )(x, *others)
-
-
-def group_stats(group_ids, rewards):
-    groups_all = GRP_ROW * lax.axis_size("grp")
+        stats_kernel,
+        in_specs=[vmem, vmem, pl.BlockSpec(memory_space=pl.ANY)],
+        out_specs=vmem,
+        out_shape=jax.ShapeDtypeStruct((copies, 1, 2 * GRP_ROW * copies), rewards.dtype),
+    )(group_ids, rewards, other)
+
+
+def advantage_of(group_ids, rewards, stats):
+    both = jnp.sum(lax.all_to_all(stats, "grp", 0, 0, tiled=True), axis=(0, 1))[None]
+    groups_all = both.shape[1] // 2
     member = group_ids[:, None] == jnp.arange(groups_all, dtype=jnp.int32)[None, :]
-    sums = jnp.sum(jnp.where(member, rewards[:, None], 0.0), axis=0)
-    counts = jnp.sum(member.astype(jnp.float32), axis=0)
-    return member, jnp.concatenate([sums, counts])[None]
-
-
-def advantage_of(member, stats, rewards):
-    rows, groups_all = lax.axis_size("grp"), member.shape[1]
-    everyone = lax.all_to_all(
-        jnp.broadcast_to(stats, (rows, stats.shape[1])), "grp", 0, 0, tiled=True
-    )
-    both = jnp.sum(everyone, axis=0)
-    own_sum = jnp.sum(jnp.where(member, both[None, :groups_all], 0.0), axis=1)
-    own_count = jnp.sum(jnp.where(member, both[None, groups_all:], 0.0), axis=1)
+    own_sum = jnp.sum(jnp.where(member, both[:, :groups_all], 0.0), axis=1)
+    own_count = jnp.sum(jnp.where(member, both[:, groups_all:], 0.0), axis=1)
     return rewards - (own_sum - rewards) / jnp.maximum(own_count - 1.0, 1.0)
 
 
@@ -199,8 +204,8 @@
         before = [dq]
         received.append((own, shifted(to_near, "ctx", -1), shifted(to_far, "ctx", -2)))
 
-    member, stats = group_stats(group_ids[0], rewards[0])
-    advantage = advantage_of(member, after(stats, *received[0][1:]), rewards[0])
+    stats = stats_after(group_ids, rewards, lax.axis_size("grp"), received[0][2])
+    advantage = advantage_of(group_ids[0], rewards[0], stats)
     picked = begun & (starts[None, :] == seg_start[:, None])
     weight = jnp.sum(jnp.where(picked, advantage[None, :], 0.0), axis=1)[:, None]
     scaled = weight * SCALE

time: 74.8 us -> 68.5 us (0.916)
  the two profiles are of different devices: /device:TPU:388 before, /device:TPU:384 now
where the time goes in v3:
time: 68.5 us; the launch traced here: 68 us
  starting transfers between devices  33.6 us (49%)
  Pallas kernels  19.6 us (29%)
  waiting for transfers between devices  7.35 us (11%)
  other arithmetic  5.44 us (8%)
  local copies, waits for them, and re-layouts  1.29 us (2%)
  between operations  0.85 us (1%)
    ppermute x8, starting transfers between devices, shifted(): return lax.ppermute(x, axis, pairs)  29.1 us
    pallas_call x2, Pallas kernels, attention_backward(): pl.pallas_call(attention_kernel, grid=(groups,), in_specs=[pl.BlockSpec(m...  18 us
    all_to_all x1, starting transfers between devices, advantage_of(): lax.all_to_all(stats, 'grp', 0, 0, tiled=True)  4.47 us
    all_to_all x1, waiting for transfers between devices, advantage_of(): lax.all_to_all(stats, 'grp', 0, 0, tiled=True)  3.7 us
    ppermute x8, waiting for transfers between devices, shifted(): return lax.ppermute(x, axis, pairs)  3.65 us
    pallas_call x1, Pallas kernels, stats_after(): pl.pallas_call(stats_kernel, in_specs=[vmem, vmem, pl.BlockSpec(memory_sp...  1.51 us
  transfers between devices with their start and end apart: 9, of which 3 were waited for; matrix products, arithmetic and copies ran while one was open for 3% of the time, Pallas kernels for 29%

profile of v3, /device:TPU:384, one launch (start us, length us, event | category | flops | bytes accessed | tf_op | source)
XLA Modules:
  0.0 68.0 jit_solution(11572619068019006389)
XLA Ops:
  0.7 1.2 %fusion.12 = (bf16[1,256,256]{2,1,0:T(8,128)(2,1)S(1)}, bf16[1,256,256]{2,1,0:T(8,128)(2,1)S(1)}, bf16[1,256,256]{2,1,0:T(8,128)(2,1)S(1)}, bf16[1,256,256]{2,1,0:T(8,128)(2,1)S(1)}) fusion(bf16[1,256,512]{2,1,0:T(8,128)(2,1)} %param.8, bf16[1,256,512]{2,1,0:T(8,128)(2,1)} %param.9), kind=kLoop, calls=%fused_computation.37 | loop fusion | bytes 1048576 | tf_op jit(solution)/shard_map/slice | solution.py:189
  1.9 3.4 %collective-permute-start.1 = (bf16[2,256,256]{2,1,0:T(8,128)(2,1)S(1)}, bf16[2,256,256]{2,1,0:T(8,128)(2,1)S(1)}, u32[]{:S(2)}, u32[]{:S(2)}) collective-permute-start(bf16[2,256,256]{2,1,0:T(8,128)(2,1)S(1)} %pad_maximum_fusion), channel_id=1, source_target_pairs={{0,8},{8,16},{16,24},{24,32},{32,40},{40,48},{48,56},{56,64},{64,7... | collective-permute-start | bytes 786440 | tf_op jit(solution)/shard_map/ppermute | solution.py:31
  5.3 4.6 %collective-permute-start = (bf16[2,256,256]{2,1,0:T(8,128)(2,1)S(1)}, bf16[2,256,256]{2,1,0:T(8,128)(2,1)S(1)}, u32[]{:S(2)}, u32[]{:S(2)}) collective-permute-start(bf16[2,256,256]{2,1,0:T(8,128)(2,1)S(1)} %pad_maximum_fusion), channel_id=1, source_target_pairs={{0,16},{8,24},{16,32},{24,40},{32,48},{40,56},{48,64},{56,72},{64,... | collective-permute-start | bytes 786440 | tf_op jit(solution)/shard_map/ppermute | solution.py:31
  9.9 0.7 %pad_maximum_fusion.1 = bf16[2,256,256]{2,1,0:T(8,128)(2,1)} fusion(bf16[1,256,256]{2,1,0:T(8,128)(2,1)S(1)} %get-tuple-element.34, bf16[1,256,256]{2,1,0:T(8,128)(2,1)S(1)} %get-tuple-element.25), kind=kLoop, calls=%fused_computation.17 | loop fusion | flops 131072 | bytes 524288 | tf_op jit(solution)/shard_map/stack | solution.py:189
  10.7 2.2 %collective-permute-start.3 = (bf16[2,256,256]{2,1,0:T(8,128)(2,1)}, bf16[2,256,256]{2,1,0:T(8,128)(2,1)S(1)}, u32[]{:S(2)}, u32[]{:S(2)}) collective-permute-start(bf16[2,256,256]{2,1,0:T(8,128)(2,1)} %pad_maximum_fusion.1), channel_id=1, source_target_pairs={{0,8},{8,16},{16,24},{24,32},{32,40},{40,48},{48,56},{56,64},{64,7... | collective-permute-start | bytes 786440 | tf_op jit(solution)/shard_map/ppermute | solution.py:31
  12.9 4.9 %collective-permute-start.2 = (bf16[2,256,256]{2,1,0:T(8,128)(2,1)}, bf16[2,256,256]{2,1,0:T(8,128)(2,1)S(1)}, u32[]{:S(2)}, u32[]{:S(2)}) collective-permute-start(bf16[2,256,256]{2,1,0:T(8,128)(2,1)} %pad_maximum_fusion.1), channel_id=1, source_target_pairs={{0,16},{8,24},{16,32},{24,40},{32,48},{40,56},{48,64},{56,72},{64,... | collective-permute-start | bytes 786440 | tf_op jit(solution)/shard_map/ppermute | solution.py:31
  17.9 0.2 reduce-window_clone.1
  18.1 0.1 fusion.9
  18.2 0.0 collective-permute-done.1.refs_1_
  18.2 3.3 %collective-permute-done.refs_0_ = bf16[2,256,256]{2,1,0:T(8,128)(2,1)S(1)} collective-permute-done((bf16[2,256,256]{2,1,0:T(8,128)(2,1)S(1)}, bf16[2,256,256]{2,1,0:T(8,128)(2,1)S(1)}, u32[]{:S(2)}, u32[]{:S(2)}) %collective-permute-start) | collective-permute-done | bytes 262176 | tf_op jit(solution)/shard_map/ppermute | solution.py:31
  21.5 9.0 %shard_map.94 = (bf16[256,2560]{1,0:T(8,128)(2,1)S(1)}, f32[2,256,256]{2,1,0:T(8,128)S(1)}, bf16[2,256,256]{2,1,0:T(8,128)(2,1)}, bf16[2,256,256]{2,1,0:T(8,128)(2,1)S(1)}) custom-call(bf16[2,256,256]{2,1,0:T(8,128)(2,1)S(1)} %collective-permute-done.refs_0_, bf16[2,256,256]{2,1,0:T(8,128)(2,1)S(1)} %collective-permute-done.1.refs_1_, ...), custom_call_target="tpu_custom_call" | custom-call | flops 8000000000 | bytes 4194304 | tf_op jit(solution)/shard_map/pallas_call | solution.py:112
  30.5 3.7 %collective-permute-start.4 = (bf16[2,256,256]{2,1,0:T(8,128)(2,1)S(1)}, bf16[2,256,256]{2,1,0:T(8,128)(2,1)}, u32[]{:S(2)}, u32[]{:S(2)}) collective-permute-start(bf16[2,256,256]{2,1,0:T(8,128)(2,1)S(1)} %get-tuple-element.13), channel_id=1, source_target_pairs={{16,0},{24,8},{32,16},{40,24},{48,32},{56,40},{64,48},{72,56},{80,... | collective-permute-start | bytes 786440 | tf_op jit(solution)/shard_map/ppermute | solution.py:31
  34.2 4.6 %collective-permute-start.5 = (bf16[2,256,256]{2,1,0:T(8,128)(2,1)}, bf16[2,256,256]{2,1,0:T(8,128)(2,1)}, u32[]{:S(2)}, u32[]{:S(2)}) collective-permute-start(bf16[2,256,256]{2,1,0:T(8,128)(2,1)} %get-tuple-element.15), channel_id=1, source_target_pairs={{8,0},{16,8},{24,16},{32,24},{40,32},{48,40},{56,48},{64,56},{72,6... | collective-permute-start | bytes 786440 | tf_op jit(solution)/shard_map/ppermute | solution.py:31
  38.8 0.0 collective-permute-done.3.refs_2_
  38.8 9.0 %shard_map.95 = (bf16[256,2560]{1,0:T(8,128)(2,1)S(1)}, f32[2,256,256]{2,1,0:T(8,128)S(1)}, bf16[2,256,256]{2,1,0:T(8,128)(2,1)}, bf16[2,256,256]{2,1,0:T(8,128)(2,1)}) custom-call(bf16[256,2560]{1,0:T(8,128)(2,1)S(1)} %get-tuple-element.11.refs_0_, bf16[2,256,256]{2,1,0:T(8,128)(2,1)S(1)} %collective-permute-done.2.refs_1_, ...), custom_call_target="tpu_custom_call", output_to_operand_aliasing={{0}: (0, {})} | custom-call | flops 8000000000 | bytes 4194304 | tf_op jit(solution)/shard_map/pallas_call | solution.py:112
  47.8 2.4 %collective-permute-start.6 = (bf16[2,256,256]{2,1,0:T(8,128)(2,1)}, bf16[2,256,256]{2,1,0:T(8,128)(2,1)S(1)}, u32[]{:S(2)}, u32[]{:S(2)}) collective-permute-start(bf16[2,256,256]{2,1,0:T(8,128)(2,1)} %get-tuple-element.17), channel_id=1, source_target_pairs={{8,0},{16,8},{24,16},{32,24},{40,32},{48,40},{56,48},{64,56},{72,6... | collective-permute-start | bytes 786440 | tf_op jit(solution)/shard_map/ppermute | solution.py:31
  50.2 3.3 %collective-permute-start.7 = (bf16[2,256,256]{2,1,0:T(8,128)(2,1)}, bf16[2,256,256]{2,1,0:T(8,128)(2,1)S(1)}, u32[]{:S(2)}, u32[]{:S(2)}) collective-permute-start(bf16[2,256,256]{2,1,0:T(8,128)(2,1)} %get-tuple-element.18), channel_id=1, source_target_pairs={{16,0},{24,8},{32,16},{40,24},{48,32},{56,40},{64,48},{72,56},{80,... | collective-permute-start | bytes 786440 | tf_op jit(solution)/shard_map/ppermute | solution.py:31
  53.5 1.5 %shard_map.96 = f32[8,1,64]{2,1,0:T(1,128)} custom-call(s32[1,64]{1,0:T(1,128)} %ids_ref.1, f32[1,64]{1,0:T(1,128)} %rewards_ref.1, bf16[2,256,256]{2,1,0:T(8,128)(2,1)} %collective-permute-done.4._), custom_call_target="tpu_custom_call" | custom-call | tf_op jit(solution)/shard_map/pallas_call | solution.py:167
  55.1 4.5 %all-to-all-start = ((f32[8,1,64]{2,1,0:T(1,128)}), f32[8,1,64]{2,1,0:T(1,128)S(1)}, u32[]{:S(2)}, u32[]{:S(2)}) async-start(f32[8,1,64]{2,1,0:T(1,128)} %shard_map.96), calls=%async_computation | async-start | bytes 8192 | tf_op jit(solution)/shard_map/all_to_all | solution.py:176
  59.5 0.0 copy-start.2
  59.5 0.0 copy-start.3
  59.6 1.1 %convert_add_fusion.1 = f32[2,256,256]{2,1,0:T(8,128)S(1)} fusion(bf16[2,256,256]{2,1,0:T(8,128)(2,1)} %collective-permute-done.4._, f32[2,256,256]{2,1,0:T(8,128)S(1)} %get-tuple-element.14, bf16[2,256,256]{2,1,0:T(8,128)(2,1)} %collective-permute-done.5), kind=kLoop, calls=%fused_computation.3 | loop fusion | flops 524288 | bytes 1572864 | tf_op jit(solution)/shard_map/add | solution.py:213
  60.7 0.3 collective-permute-done.6
  61.0 0.1 convert_add_fusion
  61.1 3.7 %all-to-all-done = f32[8,1,64]{2,1,0:T(1,128)S(1)} async-done(((f32[8,1,64]{2,1,0:T(1,128)}), f32[8,1,64]{2,1,0:T(1,128)S(1)}, u32[]{:S(2)}, u32[]{:S(2)}) %all-to-all-start) | async-done | bytes 2080 | tf_op jit(solution)/shard_map/all_to_all | solution.py:176
  64.8 0.1 slice_bitcast_fusion.4
  64.9 0.1 select_reduce_fusion.2
  65.0 0.1 select_reduce_fusion
  65.1 1.3 %fusion = bf16[1,256,2560]{2,1,0:T(8,128)(2,1)} fusion(bf16[256,2560]{1,0:T(8,128)(2,1)S(1)} %get-tuple-element.12, f32[256]{0:T(256)S(1)} %broadcast_multiply_fusion), kind=kLoop, calls=%fused_computation.1 | loop fusion | flops 1966080 | bytes 2622464 | tf_op jit(solution)/shard_map/broadcast_in_dim | solution.py:216
  66.5 0.1 fusion.2
  66.6 0.7 %maximum_bitcast_fusion.1 = bf16[1,256,512]{2,1,0:T(8,128)(2,1)} fusion(bf16[256,256]{1,0:T(8,128)(2,1)S(1)} %get-tuple-element.23, bf16[256,256]{1,0:T(8,128)(2,1)S(1)} %get-tuple-element.30), kind=kLoop, calls=%fused_computation.19 | loop fusion | flops 524288 | bytes 524288 | tf_op jit(solution)/shard_map/broadcast_in_dim | solution.py:216
  67.3 0.7 %maximum_bitcast_fusion = bf16[1,256,512]{2,1,0:T(8,128)(2,1)} fusion(bf16[256,256]{1,0:T(8,128)(2,1)S(1)} %get-tuple-element.24, bf16[256,256]{1,0:T(8,128)(2,1)S(1)} %get-tuple-element.29), kind=kLoop, calls=%fused_computation.18 | loop fusion | flops 524288 | bytes 524288 | tf_op jit(solution)/shard_map/broadcast_in_dim | solution.py:216
  (19 shorter events, 0.1 us)
Async XLA Ops:
  0.6 20.9 %copy-start.1 = (bf16[1,256,512]{2,1,0:T(8,128)(2,1)S(1)}, bf16[1,256,512]{2,1,0:T(8,128)(2,1)}, u32[]{:S(2)}) copy-start(bf16[1,256,512]{2,1,0:T(8,128)(2,1)} %param.9) | copy-start | bytes 786436
  0.6 20.9 %copy-start = (bf16[1,256,512]{2,1,0:T(8,128)(2,1)S(1)}, bf16[1,256,512]{2,1,0:T(8,128)(2,1)}, u32[]{:S(2)}) copy-start(bf16[1,256,512]{2,1,0:T(8,128)(2,1)} %param.8) | copy-start | bytes 786436
  0.7 17.2 %copy-start.4 = (s32[1,64]{1,0:T(1,128)S(1)}, s32[1,64]{1,0:T(1,128)}, u32[]{:S(2)}) copy-start(s32[1,64]{1,0:T(1,128)} %param.11) | copy-start | bytes 772
  1.9 16.3 %collective-permute-start.1 = (bf16[2,256,256]{2,1,0:T(8,128)(2,1)S(1)}, bf16[2,256,256]{2,1,0:T(8,128)(2,1)S(1)}, u32[]{:S(2)}, u32[]{:S(2)}) collective-permute-start(bf16[2,256,256]{2,1,0:T(8,128)(2,1)S(1)} %pad_maximum_fusion), channel_id=1, source_target_pairs={{0,8},{8,16},{16,24},{24,32},{32,40},{40,48},{48,56},{56,64},{64,7... | collective-permute-start | bytes 786440 | tf_op jit(solution)/shard_map/ppermute | solution.py:31
  5.3 16.2 %collective-permute-start = (bf16[2,256,256]{2,1,0:T(8,128)(2,1)S(1)}, bf16[2,256,256]{2,1,0:T(8,128)(2,1)S(1)}, u32[]{:S(2)}, u32[]{:S(2)}) collective-permute-start(bf16[2,256,256]{2,1,0:T(8,128)(2,1)S(1)} %pad_maximum_fusion), channel_id=1, source_target_pairs={{0,16},{8,24},{16,32},{24,40},{32,48},{40,56},{48,64},{56,72},{64,... | collective-permute-start | bytes 786440 | tf_op jit(solution)/shard_map/ppermute | solution.py:31
  10.7 28.1 %collective-permute-start.3 = (bf16[2,256,256]{2,1,0:T(8,128)(2,1)}, bf16[2,256,256]{2,1,0:T(8,128)(2,1)S(1)}, u32[]{:S(2)}, u32[]{:S(2)}) collective-permute-start(bf16[2,256,256]{2,1,0:T(8,128)(2,1)} %pad_maximum_fusion.1), channel_id=1, source_target_pairs={{0,8},{8,16},{16,24},{24,32},{32,40},{40,48},{48,56},{56,64},{64,7... | collective-permute-start | bytes 786440 | tf_op jit(solution)/shard_map/ppermute | solution.py:31
  12.9 25.9 %collective-permute-start.2 = (bf16[2,256,256]{2,1,0:T(8,128)(2,1)}, bf16[2,256,256]{2,1,0:T(8,128)(2,1)S(1)}, u32[]{:S(2)}, u32[]{:S(2)}) collective-permute-start(bf16[2,256,256]{2,1,0:T(8,128)(2,1)} %pad_maximum_fusion.1), channel_id=1, source_target_pairs={{0,16},{8,24},{16,32},{24,40},{32,48},{40,56},{48,64},{56,72},{64,... | collective-permute-start | bytes 786440 | tf_op jit(solution)/shard_map/ppermute | solution.py:31
  30.5 23.0 %collective-permute-start.4 = (bf16[2,256,256]{2,1,0:T(8,128)(2,1)S(1)}, bf16[2,256,256]{2,1,0:T(8,128)(2,1)}, u32[]{:S(2)}, u32[]{:S(2)}) collective-permute-start(bf16[2,256,256]{2,1,0:T(8,128)(2,1)S(1)} %get-tuple-element.13), channel_id=1, source_target_pairs={{16,0},{24,8},{32,16},{40,24},{48,32},{56,40},{64,48},{72,56},{80,... | collective-permute-start | bytes 786440 | tf_op jit(solution)/shard_map/ppermute | solution.py:31
  34.2 25.3 %collective-permute-start.5 = (bf16[2,256,256]{2,1,0:T(8,128)(2,1)}, bf16[2,256,256]{2,1,0:T(8,128)(2,1)}, u32[]{:S(2)}, u32[]{:S(2)}) collective-permute-start(bf16[2,256,256]{2,1,0:T(8,128)(2,1)} %get-tuple-element.15), channel_id=1, source_target_pairs={{8,0},{16,8},{24,16},{32,24},{40,32},{48,40},{56,48},{64,56},{72,6... | collective-permute-start | bytes 786440 | tf_op jit(solution)/shard_map/ppermute | solution.py:31
  47.8 13.2 %collective-permute-start.6 = (bf16[2,256,256]{2,1,0:T(8,128)(2,1)}, bf16[2,256,256]{2,1,0:T(8,128)(2,1)S(1)}, u32[]{:S(2)}, u32[]{:S(2)}) collective-permute-start(bf16[2,256,256]{2,1,0:T(8,128)(2,1)} %get-tuple-element.17), channel_id=1, source_target_pairs={{8,0},{16,8},{24,16},{32,24},{40,32},{48,40},{56,48},{64,56},{72,6... | collective-permute-start | bytes 786440 | tf_op jit(solution)/shard_map/ppermute | solution.py:31
  50.2 10.8 %collective-permute-start.7 = (bf16[2,256,256]{2,1,0:T(8,128)(2,1)}, bf16[2,256,256]{2,1,0:T(8,128)(2,1)S(1)}, u32[]{:S(2)}, u32[]{:S(2)}) collective-permute-start(bf16[2,256,256]{2,1,0:T(8,128)(2,1)} %get-tuple-element.18), channel_id=1, source_target_pairs={{16,0},{24,8},{32,16},{40,24},{48,32},{56,40},{64,48},{72,56},{80,... | collective-permute-start | bytes 786440 | tf_op jit(solution)/shard_map/ppermute | solution.py:31
  55.1 9.7 %all-to-all-start = ((f32[8,1,64]{2,1,0:T(1,128)}), f32[8,1,64]{2,1,0:T(1,128)S(1)}, u32[]{:S(2)}, u32[]{:S(2)}) async-start(f32[8,1,64]{2,1,0:T(1,128)} %shard_map.96), calls=%async_computation | async-start | bytes 8192 | tf_op jit(solution)/shard_map/all_to_all | solution.py:176
  59.5 5.4 %copy-start.2 = (s32[1,64]{1,0:T(1,128)S(1)}, s32[1,64]{1,0:T(1,128)}, u32[]{:S(2)}) copy-start(s32[1,64]{1,0:T(1,128)} %ids_ref.1) | copy-start | bytes 772
  59.5 5.4 %copy-start.3 = (f32[1,64]{1,0:T(1,128)S(1)}, f32[1,64]{1,0:T(1,128)}, u32[]{:S(2)}) copy-start(f32[1,64]{1,0:T(1,128)} %rewards_ref.1) | copy-start | bytes 772

commit v4 on v3

--- a/solution.py
+++ b/solution.py
@@ -1,3 +1,4 @@
+import functools
 import math
 
 import jax
@@ -21,7 +22,7 @@
 EXP_SCALE = SCALE * math.log2(math.e)
 EXCLUDED = -1e30
 PARTS = 2
-VMEM_BYTES = 32 * 1024 * 1024
+VMEM_BYTES = 24 * 1024 * 1024
 COST_FLOPS = 4_000_000_000
 
 
@@ -31,7 +32,11 @@
     return lax.ppermute(x, axis, pairs)
 
 
-def attention_kernel(*refs):
+def attention_kernel(ahead, *refs):
+    if ahead:
+        for source, target in zip(refs[-20:-18], refs[-14:-12], strict=True):
+            target[...] = source[...]
+        refs = refs[:-20] + refs[-18:-14] + refs[-12:]
     far_ref, near_ref, low_ref, q_ref, u_ref, k_ref, v_ref = refs[-23:-16]
     dq_ref, own_ref, to_near_ref, to_far_ref = refs[-16:-12]
     mask, kw, vw, kt, qj, uj, s, uv, p, ds, dk, dv = refs[-12:]
@@ -50,8 +55,6 @@
         window[ROWS : 2 * ROWS] = near_ref[at]
         window[2 * ROWS :] = own[...]
     kt[...] = kw[...].T
-    dk[...] = jnp.zeros_like(dk)
-    dv[...] = jnp.zeros_like(dv)
     for j in range(2):
         first = j * HALF
         rows = slice(first, first + HALF)
@@ -87,8 +90,13 @@
                 soft = s[tile, lanes] * inverse
                 p[tile, lanes] = soft.astype(bf16)
                 ds[tile, lanes] = (soft * (uv[tile, lanes] - delta)).astype(bf16)
-        dv[keys] += jnp.dot(p[...], uj[...], preferred_element_type=f32)
-        dk[keys] += jnp.dot(ds[...], qj[...], preferred_element_type=f32)
+        for grad, left, right in ((dv, p, uj), (dk, ds, qj)):
+            part = jnp.dot(left[...], right[...], preferred_element_type=f32)
+            if j == 0:
+                grad[:REACH] = part
+            else:
+                grad[HALF:REACH] += part[: REACH - HALF]
+                grad[REACH:] = part[REACH - HALF :]
         dq_t = jnp.dot(kt[:, keys], ds[...], preferred_element_type=f32)
         for h in range(PER):
             block = dq_t[:, h * HALF : (h + 1) * HALF]
@@ -99,28 +107,36 @@
         own_ref[at] = grad[2 * ROWS :]
 
 
-def attention_backward(part, low, q, u, k, v, near, far, before):
+def attention_backward(part, low, q, u, taken, k, v, near, far, before):
     f32, bf16 = jnp.float32, jnp.bfloat16
     groups = far.shape[2] // HEAD
-    q, u = (pltpu.with_memory_space_constraint(x, pltpu.HBM) for x in (q, u))
-    first = part * groups
+    first, after = part * groups, (part + 1) * groups
+    hbm = [pltpu.with_memory_space_constraint(x, pltpu.HBM) for x in (q, u)]
+    ahead = 2 * (part < PARTS - 1)
     row = pl.BlockSpec((1, ROWS), lambda g: (0, 0))
     wide = pl.BlockSpec((ROWS, PER * HEAD), lambda g: (0, first + g))
+    wide_part = pl.BlockSpec((ROWS, PER * HEAD), lambda g: (0, g))
+    wide_next = pl.BlockSpec((ROWS, PER * HEAD), lambda g: (0, after + g))
     head = pl.BlockSpec((ROWS, HEAD), lambda g: (0, first + g))
     pair = pl.BlockSpec((2, ROWS, HEAD), lambda g: (0, 0, g))
     pair_shape = (2, ROWS, groups * HEAD)
+    part_shape = jax.ShapeDtypeStruct((ROWS, groups * PER * HEAD), bf16)
     return pl.pallas_call(
-        attention_kernel,
+        functools.partial(attention_kernel, ahead),
         grid=(groups,),
         in_specs=[pl.BlockSpec(memory_space=pl.ANY)] * len(before)
-        + [pair, pair, row, wide, wide, head, head],
-        out_specs=[wide, pair, pair, pair],
+        + [pair, pair, row]
+        + [wide_part if taken else wide] * 2
+        + [head, head]
+        + [wide_next] * ahead,
+        out_specs=[wide, pair, pair, pair] + [wide_part] * ahead,
         out_shape=[
             jax.ShapeDtypeStruct(q.shape, bf16),
             jax.ShapeDtypeStruct(pair_shape, f32),
             jax.ShapeDtypeStruct(pair_shape, bf16),
             jax.ShapeDtypeStruct(pair_shape, bf16),
-        ],
+        ]
+        + [part_shape] * ahead,
         scratch_shapes=[
             pltpu.VMEM((2, REACH, HALF), f32),
             pltpu.VMEM((WINDOW, HEAD), bf16),
@@ -142,7 +158,7 @@
             bytes_accessed=4 * 1024 * 1024,
             transcendentals=groups * 2 * REACH * REACH,
         ),
-    )(*before, far, near, low, q, u, k, v)
+    )(*before, far, near, low, *(taken or hbm), k, v, *hbm[:ahead])
 
 
 def stats_kernel(ids_ref, rewards_ref, _, out_ref):
@@ -196,24 +212,26 @@
     seg_start = jnp.max(jnp.where(begun, starts[None, :], 0), axis=1)
     low = (seg_start - (first_row - SPAN * ROWS))[None]
 
-    before, received = [], []
+    before, taken, received = [], [], []
     for part, (near, far) in enumerate(halos):
-        dq, own, to_near, to_far = attention_backward(
-            part, low, queries[0], upstream[0], keys[0], values[0], near, far, before
+        dq, own, to_near, to_far, *taken = attention_backward(
+            part, low, queries[0], upstream[0], taken, keys[0], values[0], near, far, before
         )
         before = [dq]
-        received.append((own, shifted(to_near, "ctx", -1), shifted(to_far, "ctx", -2)))
-
-    stats = stats_after(group_ids, rewards, lax.axis_size("grp"), received[0][2])
+        received.append((own, shifted(to_far, "ctx", -2), shifted(to_near, "ctx", -1)))
+
+    stats = stats_after(group_ids, rewards, lax.axis_size("grp"), received[0][1])
     advantage = advantage_of(group_ids[0], rewards[0], stats)
     picked = begun & (starts[None, :] == seg_start[:, None])
     weight = jnp.sum(jnp.where(picked, advantage[None, :], 0.0), axis=1)[:, None]
     scaled = weight * SCALE
     dq = (dq.astype(jnp.float32) * scaled).astype(jnp.bfloat16)
-    totals = [own + a.astype(jnp.float32) + b.astype(jnp.float32) for own, a, b in received]
-    dk = [(t[0] * scaled).astype(jnp.bfloat16) for t in totals]
-    dv = [(t[1] * weight).astype(jnp.bfloat16) for t in totals]
-    return (dq[None], jnp.concatenate(dk, axis=1)[None], jnp.concatenate(dv, axis=1)[None])
+    total = jnp.concatenate(
+        [own + a.astype(jnp.float32) + b.astype(jnp.float32) for own, a, b in received], axis=2
+    )
+    dk = (total[0] * scaled).astype(jnp.bfloat16)
+    dv = (total[1] * weight).astype(jnp.bfloat16)
+    return (dq[None], dk[None], dv[None])
 
 
 def solution(mesh):

time: 68.5 us -> 68 us (level)
    broadcast_in_dim x3 -> x1, other arithmetic: 2.78 us -> 1.34 us  [local(): return (dq[None], dk[None], dv[None])]
    convert_element_type x1, other arithmetic: 0.13 us -> 0.93 us  [local(): dv = (total[1] * weight).astype(jnp.bfloat16)]
  transfers between devices with their start and end apart: 9 -> 9, of which waited for: 3 -> 2; matrix products, arithmetic and copies ran while one was open for 3% -> 3% of each run, Pallas kernels for 29% -> 28%
where the time goes in v4:
time: 68 us; the launch traced here: 67.5 us
  starting transfers between devices  34.2 us (50%)
  Pallas kernels  19.1 us (28%)
  waiting for transfers between devices  7.33 us (11%)
  other arithmetic  4.79 us (7%)
  local copies, waits for them, and re-layouts  1.29 us (2%)
  between operations  0.86 us (1%)
    ppermute x8, starting transfers between devices, shifted(): return lax.ppermute(x, axis, pairs)  29.7 us
    pallas_call x2, Pallas kernels, attention_backward(): pl.pallas_call(functools.partial(attention_kernel, ahead), grid=(groups,)...  17.6 us
    all_to_all x1, starting transfers between devices, advantage_of(): lax.all_to_all(stats, 'grp', 0, 0, tiled=True)  4.47 us
    all_to_all x1, waiting for transfers between devices, advantage_of(): lax.all_to_all(stats, 'grp', 0, 0, tiled=True)  4.02 us
    ppermute x8, waiting for transfers between devices, shifted(): return lax.ppermute(x, axis, pairs)  3.31 us
    pallas_call x1, Pallas kernels, stats_after(): pl.pallas_call(stats_kernel, in_specs=[vmem, vmem, pl.BlockSpec(memory_sp...  1.51 us
  transfers between devices with their start and end apart: 9, of which 2 were waited for; matrix products, arithmetic and copies ran while one was open for 3% of the time, Pallas kernels for 28%

profile of v4, /device:TPU:384, one launch (start us, length us, event | category | flops | bytes accessed | tf_op | source)
XLA Modules:
  0.0 67.5 jit_solution(10904608156575310796)
XLA Ops:
  0.7 1.2 %fusion.9 = (bf16[1,256,256]{2,1,0:T(8,128)(2,1)S(1)}, bf16[1,256,256]{2,1,0:T(8,128)(2,1)S(1)}, bf16[1,256,256]{2,1,0:T(8,128)(2,1)S(1)}, bf16[1,256,256]{2,1,0:T(8,128)(2,1)S(1)}) fusion(bf16[1,256,512]{2,1,0:T(8,128)(2,1)} %param.8, bf16[1,256,512]{2,1,0:T(8,128)(2,1)} %param.9), kind=kLoop, calls=%fused_computation.31 | loop fusion | bytes 1048576 | tf_op jit(solution)/shard_map/slice | solution.py:205
  1.9 3.4 %collective-permute-start.1 = (bf16[2,256,256]{2,1,0:T(8,128)(2,1)S(1)}, bf16[2,256,256]{2,1,0:T(8,128)(2,1)S(1)}, u32[]{:S(2)}, u32[]{:S(2)}) collective-permute-start(bf16[2,256,256]{2,1,0:T(8,128)(2,1)S(1)} %pad_maximum_fusion.1), channel_id=1, source_target_pairs={{0,8},{8,16},{16,24},{24,32},{32,40},{40,48},{48,56},{56,64},{64,7... | collective-permute-start | bytes 786440 | tf_op jit(solution)/shard_map/ppermute | solution.py:32
  5.3 4.6 %collective-permute-start = (bf16[2,256,256]{2,1,0:T(8,128)(2,1)S(1)}, bf16[2,256,256]{2,1,0:T(8,128)(2,1)S(1)}, u32[]{:S(2)}, u32[]{:S(2)}) collective-permute-start(bf16[2,256,256]{2,1,0:T(8,128)(2,1)S(1)} %pad_maximum_fusion.1), channel_id=1, source_target_pairs={{0,16},{8,24},{16,32},{24,40},{32,48},{40,56},{48,64},{56,72},{64,... | collective-permute-start | bytes 786440 | tf_op jit(solution)/shard_map/ppermute | solution.py:32
  9.9 0.7 %pad_maximum_fusion.2 = bf16[2,256,256]{2,1,0:T(8,128)(2,1)} fusion(bf16[1,256,256]{2,1,0:T(8,128)(2,1)S(1)} %get-tuple-element.34, bf16[1,256,256]{2,1,0:T(8,128)(2,1)S(1)} %get-tuple-element.27), kind=kLoop, calls=%fused_computation.13 | loop fusion | flops 131072 | bytes 524288 | tf_op jit(solution)/shard_map/stack | solution.py:205
  10.7 2.2 %collective-permute-start.3 = (bf16[2,256,256]{2,1,0:T(8,128)(2,1)}, bf16[2,256,256]{2,1,0:T(8,128)(2,1)S(1)}, u32[]{:S(2)}, u32[]{:S(2)}) collective-permute-start(bf16[2,256,256]{2,1,0:T(8,128)(2,1)} %pad_maximum_fusion.2), channel_id=1, source_target_pairs={{0,8},{8,16},{16,24},{24,32},{32,40},{40,48},{48,56},{56,64},{64,7... | collective-permute-start | bytes 786440 | tf_op jit(solution)/shard_map/ppermute | solution.py:32
  12.9 4.9 %collective-permute-start.2 = (bf16[2,256,256]{2,1,0:T(8,128)(2,1)}, bf16[2,256,256]{2,1,0:T(8,128)(2,1)S(1)}, u32[]{:S(2)}, u32[]{:S(2)}) collective-permute-start(bf16[2,256,256]{2,1,0:T(8,128)(2,1)} %pad_maximum_fusion.2), channel_id=1, source_target_pairs={{0,16},{8,24},{16,32},{24,40},{32,48},{40,56},{48,64},{56,72},{64,... | collective-permute-start | bytes 786440 | tf_op jit(solution)/shard_map/ppermute | solution.py:32
  17.9 0.2 reduce-window_clone.1
  18.1 0.1 fusion.6
  18.2 0.0 collective-permute-done.1.refs_1_
  18.2 3.3 %collective-permute-done.refs_0_ = bf16[2,256,256]{2,1,0:T(8,128)(2,1)S(1)} collective-permute-done((bf16[2,256,256]{2,1,0:T(8,128)(2,1)S(1)}, bf16[2,256,256]{2,1,0:T(8,128)(2,1)S(1)}, u32[]{:S(2)}, u32[]{:S(2)}) %collective-permute-start) | collective-permute-done | bytes 262176 | tf_op jit(solution)/shard_map/ppermute | solution.py:32
  21.5 9.4 %shard_map.94 = (bf16[256,2560]{1,0:T(8,128)(2,1)S(1)}, f32[2,256,256]{2,1,0:T(8,128)S(1)}, bf16[2,256,256]{2,1,0:T(8,128)(2,1)}, bf16[2,256,256]{2,1,0:T(8,128)...) custom-call(bf16[2,256,256]{2,1,0:T(8,128)(2,1)S(1)} %collective-permute-done.refs_0_, ...), custom_call_target="tpu_custom_call" | custom-call | flops 8000000000 | bytes 4194304 | tf_op jit(solution)/shard_map/pallas_call | solution.py:124
  30.9 3.7 %collective-permute-start.4 = (bf16[2,256,256]{2,1,0:T(8,128)(2,1)S(1)}, bf16[2,256,256]{2,1,0:T(8,128)(2,1)}, u32[]{:S(2)}, u32[]{:S(2)}) collective-permute-start(bf16[2,256,256]{2,1,0:T(8,128)(2,1)S(1)} %get-tuple-element.17), channel_id=1, source_target_pairs={{16,0},{24,8},{32,16},{40,24},{48,32},{56,40},{64,48},{72,56},{80,... | collective-permute-start | bytes 786440 | tf_op jit(solution)/shard_map/ppermute | solution.py:32
  34.6 4.6 %collective-permute-start.5 = (bf16[2,256,256]{2,1,0:T(8,128)(2,1)}, bf16[2,256,256]{2,1,0:T(8,128)(2,1)}, u32[]{:S(2)}, u32[]{:S(2)}) collective-permute-start(bf16[2,256,256]{2,1,0:T(8,128)(2,1)} %get-tuple-element.19), channel_id=1, source_target_pairs={{8,0},{16,8},{24,16},{32,24},{40,32},{48,40},{56,48},{64,56},{72,6... | collective-permute-start | bytes 786440 | tf_op jit(solution)/shard_map/ppermute | solution.py:32
  39.1 0.0 collective-permute-done.3.refs_2_
  39.2 0.0 collective-permute-done.2.refs_1_
  39.2 8.2 %shard_map.95 = (bf16[256,2560]{1,0:T(8,128)(2,1)S(1)}, f32[2,256,256]{2,1,0:T(8,128)S(1)}, bf16[2,256,256]{2,1,0:T(8,128)(2,1)}, bf16[2,256,256]{2,1,0:T(8,128)(2,1)}) custom-call(bf16[256,2560]{1,0:T(8,128)(2,1)S(1)} %get-tuple-element.13.refs_0_, bf16[2,256,256]{2,1,0:T(8,128)(2,1)S(1)} %collective-permute-done.2.refs_1_, ...), custom_call_target="tpu_custom_call", output_to_operand_aliasing={{0}: (0, {})} | custom-call | flops 8000000000 | bytes 4194304 | tf_op jit(solution)/shard_map/pallas_call | solution.py:124
  47.4 3.3 %collective-permute-start.6 = (bf16[2,256,256]{2,1,0:T(8,128)(2,1)}, bf16[2,256,256]{2,1,0:T(8,128)(2,1)S(1)}, u32[]{:S(2)}, u32[]{:S(2)}) collective-permute-start(bf16[2,256,256]{2,1,0:T(8,128)(2,1)} %get-tuple-element.21), channel_id=1, source_target_pairs={{16,0},{24,8},{32,16},{40,24},{48,32},{56,40},{64,48},{72,56},{80,... | collective-permute-start | bytes 786440 | tf_op jit(solution)/shard_map/ppermute | solution.py:32
  50.7 3.0 %collective-permute-start.7 = (bf16[2,256,256]{2,1,0:T(8,128)(2,1)}, bf16[2,256,256]{2,1,0:T(8,128)(2,1)S(1)}, u32[]{:S(2)}, u32[]{:S(2)}) collective-permute-start(bf16[2,256,256]{2,1,0:T(8,128)(2,1)} %get-tuple-element.22), channel_id=1, source_target_pairs={{8,0},{16,8},{24,16},{32,24},{40,32},{48,40},{56,48},{64,56},{72,6... | collective-permute-start | bytes 786440 | tf_op jit(solution)/shard_map/ppermute | solution.py:32
  53.7 1.5 %shard_map.96 = f32[8,1,64]{2,1,0:T(1,128)} custom-call(s32[1,64]{1,0:T(1,128)} %ids_ref.1, f32[1,64]{1,0:T(1,128)} %rewards_ref.1, bf16[2,256,256]{2,1,0:T(8,128)(2,1)} %collective-permute-done.4._), custom_call_target="tpu_custom_call" | custom-call | tf_op jit(solution)/shard_map/pallas_call | solution.py:183
  55.2 4.5 %all-to-all-start = ((f32[8,1,64]{2,1,0:T(1,128)}), f32[8,1,64]{2,1,0:T(1,128)S(1)}, u32[]{:S(2)}, u32[]{:S(2)}) async-start(f32[8,1,64]{2,1,0:T(1,128)} %shard_map.96), calls=%async_computation | async-start | bytes 8192 | tf_op jit(solution)/shard_map/all_to_all | solution.py:192
  59.7 0.0 collective-permute-done.5
  59.7 0.0 copy-start.2
  59.7 0.0 copy-start.3
  59.7 1.1 %convert_add_fusion.1 = f32[2,256,256]{2,1,0:T(8,128)S(1)} fusion(bf16[2,256,256]{2,1,0:T(8,128)(2,1)} %collective-permute-done.5, f32[2,256,256]{2,1,0:T(8,128)S(1)} %get-tuple-element.18, bf16[2,256,256]{2,1,0:T(8,128)(2,1)} %collective-permute-done.4._), kind=kLoop, calls=%fused_computation.11 | loop fusion | flops 524288 | bytes 1572864 | tf_op jit(solution)/shard_map/add | solution.py:230
  60.8 0.0 collective-permute-done.7
  60.9 0.1 convert_add_fusion
  60.9 4.0 %all-to-all-done = f32[8,1,64]{2,1,0:T(1,128)S(1)} async-done(((f32[8,1,64]{2,1,0:T(1,128)}), f32[8,1,64]{2,1,0:T(1,128)S(1)}, u32[]{:S(2)}, u32[]{:S(2)}) %all-to-all-start) | async-done | bytes 2080 | tf_op jit(solution)/shard_map/all_to_all | solution.py:192
  65.0 0.1 slice_bitcast_fusion
  65.1 0.1 select_reduce_fusion.2
  65.2 0.1 select_reduce_fusion
  65.3 1.3 %fusion = bf16[1,256,2560]{2,1,0:T(8,128)(2,1)} fusion(bf16[256,2560]{1,0:T(8,128)(2,1)S(1)} %get-tuple-element.16, f32[256]{0:T(256)S(1)} %broadcast_multiply_fusion), kind=kLoop, calls=%fused_computation.1 | loop fusion | flops 1966080 | bytes 2622464 | tf_op jit(solution)/shard_map/broadcast_in_dim | solution.py:234
  66.6 0.9 %fusion.5 = (bf16[1,256,512]{2,1,0:T(8,128)(2,1)}, bf16[1,256,512]{2,1,0:T(8,128)(2,1)}) fusion(f32[2,256,256]{2,1,0:T(8,128)S(1)} %convert_add_fusion, f32[2,256,256]{2,1,0:T(8,128)S(1)} %convert_add_fusion.1, f32[256]{0:T(256)S(1)} %select_reduce_fusion, f32[256]{0:T(256)S(1)} %broadcast_multiply_fusion), kind=kLoop, calls=%fused_computation.9 | loop fusion | flops 786432 | bytes 1574912 | tf_op jit(solution)/shard_map/convert_element_type | solution.py:233
  (17 shorter events, 0.1 us)
Async XLA Ops:
  0.6 20.9 %copy-start.1 = (bf16[1,256,512]{2,1,0:T(8,128)(2,1)S(1)}, bf16[1,256,512]{2,1,0:T(8,128)(2,1)}, u32[]{:S(2)}) copy-start(bf16[1,256,512]{2,1,0:T(8,128)(2,1)} %param.9) | copy-start | bytes 786436
  0.6 20.9 %copy-start = (bf16[1,256,512]{2,1,0:T(8,128)(2,1)S(1)}, bf16[1,256,512]{2,1,0:T(8,128)(2,1)}, u32[]{:S(2)}) copy-start(bf16[1,256,512]{2,1,0:T(8,128)(2,1)} %param.8) | copy-start | bytes 786436
  0.7 17.2 %copy-start.4 = (s32[1,64]{1,0:T(1,128)S(1)}, s32[1,64]{1,0:T(1,128)}, u32[]{:S(2)}) copy-start(s32[1,64]{1,0:T(1,128)} %param.11) | copy-start | bytes 772
  1.9 16.3 %collective-permute-start.1 = (bf16[2,256,256]{2,1,0:T(8,128)(2,1)S(1)}, bf16[2,256,256]{2,1,0:T(8,128)(2,1)S(1)}, u32[]{:S(2)}, u32[]{:S(2)}) collective-permute-start(bf16[2,256,256]{2,1,0:T(8,128)(2,1)S(1)} %pad_maximum_fusion.1), channel_id=1, source_target_pairs={{0,8},{8,16},{16,24},{24,32},{32,40},{40,48},{48,56},{56,64},{64,7... | collective-permute-start | bytes 786440 | tf_op jit(solution)/shard_map/ppermute | solution.py:32
  5.3 16.2 %collective-permute-start = (bf16[2,256,256]{2,1,0:T(8,128)(2,1)S(1)}, bf16[2,256,256]{2,1,0:T(8,128)(2,1)S(1)}, u32[]{:S(2)}, u32[]{:S(2)}) collective-permute-start(bf16[2,256,256]{2,1,0:T(8,128)(2,1)S(1)} %pad_maximum_fusion.1), channel_id=1, source_target_pairs={{0,16},{8,24},{16,32},{24,40},{32,48},{40,56},{48,64},{56,72},{64,... | collective-permute-start | bytes 786440 | tf_op jit(solution)/shard_map/ppermute | solution.py:32
  10.7 28.5 %collective-permute-start.3 = (bf16[2,256,256]{2,1,0:T(8,128)(2,1)}, bf16[2,256,256]{2,1,0:T(8,128)(2,1)S(1)}, u32[]{:S(2)}, u32[]{:S(2)}) collective-permute-start(bf16[2,256,256]{2,1,0:T(8,128)(2,1)} %pad_maximum_fusion.2), channel_id=1, source_target_pairs={{0,8},{8,16},{16,24},{24,32},{32,40},{40,48},{48,56},{56,64},{64,7... | collective-permute-start | bytes 786440 | tf_op jit(solution)/shard_map/ppermute | solution.py:32
  12.9 26.3 %collective-permute-start.2 = (bf16[2,256,256]{2,1,0:T(8,128)(2,1)}, bf16[2,256,256]{2,1,0:T(8,128)(2,1)S(1)}, u32[]{:S(2)}, u32[]{:S(2)}) collective-permute-start(bf16[2,256,256]{2,1,0:T(8,128)(2,1)} %pad_maximum_fusion.2), channel_id=1, source_target_pairs={{0,16},{8,24},{16,32},{24,40},{32,48},{40,56},{48,64},{56,72},{64,... | collective-permute-start | bytes 786440 | tf_op jit(solution)/shard_map/ppermute | solution.py:32
  30.9 22.8 %collective-permute-start.4 = (bf16[2,256,256]{2,1,0:T(8,128)(2,1)S(1)}, bf16[2,256,256]{2,1,0:T(8,128)(2,1)}, u32[]{:S(2)}, u32[]{:S(2)}) collective-permute-start(bf16[2,256,256]{2,1,0:T(8,128)(2,1)S(1)} %get-tuple-element.17), channel_id=1, source_target_pairs={{16,0},{24,8},{32,16},{40,24},{48,32},{56,40},{64,48},{72,56},{80,... | collective-permute-start | bytes 786440 | tf_op jit(solution)/shard_map/ppermute | solution.py:32
  34.6 25.1 %collective-permute-start.5 = (bf16[2,256,256]{2,1,0:T(8,128)(2,1)}, bf16[2,256,256]{2,1,0:T(8,128)(2,1)}, u32[]{:S(2)}, u32[]{:S(2)}) collective-permute-start(bf16[2,256,256]{2,1,0:T(8,128)(2,1)} %get-tuple-element.19), channel_id=1, source_target_pairs={{8,0},{16,8},{24,16},{32,24},{40,32},{48,40},{56,48},{64,56},{72,6... | collective-permute-start | bytes 786440 | tf_op jit(solution)/shard_map/ppermute | solution.py:32
  47.4 13.4 %collective-permute-start.6 = (bf16[2,256,256]{2,1,0:T(8,128)(2,1)}, bf16[2,256,256]{2,1,0:T(8,128)(2,1)S(1)}, u32[]{:S(2)}, u32[]{:S(2)}) collective-permute-start(bf16[2,256,256]{2,1,0:T(8,128)(2,1)} %get-tuple-element.21), channel_id=1, source_target_pairs={{16,0},{24,8},{32,16},{40,24},{48,32},{56,40},{64,48},{72,56},{80,... | collective-permute-start | bytes 786440 | tf_op jit(solution)/shard_map/ppermute | solution.py:32
  50.7 10.1 %collective-permute-start.7 = (bf16[2,256,256]{2,1,0:T(8,128)(2,1)}, bf16[2,256,256]{2,1,0:T(8,128)(2,1)S(1)}, u32[]{:S(2)}, u32[]{:S(2)}) collective-permute-start(bf16[2,256,256]{2,1,0:T(8,128)(2,1)} %get-tuple-element.22), channel_id=1, source_target_pairs={{8,0},{16,8},{24,16},{32,24},{40,32},{48,40},{56,48},{64,56},{72,6... | collective-permute-start | bytes 786440 | tf_op jit(solution)/shard_map/ppermute | solution.py:32
  55.2 9.7 %all-to-all-start = ((f32[8,1,64]{2,1,0:T(1,128)}), f32[8,1,64]{2,1,0:T(1,128)S(1)}, u32[]{:S(2)}, u32[]{:S(2)}) async-start(f32[8,1,64]{2,1,0:T(1,128)} %shard_map.96), calls=%async_computation | async-start | bytes 8192 | tf_op jit(solution)/shard_map/all_to_all | solution.py:192
  59.7 5.4 %copy-start.2 = (s32[1,64]{1,0:T(1,128)S(1)}, s32[1,64]{1,0:T(1,128)}, u32[]{:S(2)}) copy-start(s32[1,64]{1,0:T(1,128)} %ids_ref.1) | copy-start | bytes 772
  59.7 5.4 %copy-start.3 = (f32[1,64]{1,0:T(1,128)S(1)}, f32[1,64]{1,0:T(1,128)}, u32[]{:S(2)}) copy-start(f32[1,64]{1,0:T(1,128)} %rewards_ref.1) | copy-start | bytes 772

commit v5 on v4

--- a/solution.py
+++ b/solution.py
@@ -161,31 +161,22 @@
     )(*before, far, near, low, *(taken or hbm), k, v, *hbm[:ahead])
 
 
-def stats_kernel(ids_ref, rewards_ref, _, out_ref):
-    copies, groups_all = out_ref.shape[0], out_ref.shape[2] // 2
-    ids = jnp.broadcast_to(ids_ref[...], (groups_all, ids_ref.shape[1]))
-    member = (ids == lax.broadcasted_iota(jnp.int32, ids.shape, 0)).astype(jnp.float32)
-    rewards = jnp.broadcast_to(rewards_ref[...], (copies, ids.shape[1]))
-    sums, counts = (
-        lax.dot_general(
-            x, member, (((1,), (1,)), ((), ())),
-            precision=lax.Precision.HIGHEST, preferred_element_type=jnp.float32,
-        )
-        for x in (rewards, jnp.ones_like(rewards))
-    )
-    stats = jnp.concatenate([sums, counts], axis=1)
-    for i in range(copies):
-        out_ref[i] = stats[i : i + 1]
+def spread_kernel(x_ref, _, out_ref):
+    out_ref[...] = jnp.broadcast_to(x_ref[...][None], out_ref.shape)
 
 
 def stats_after(group_ids, rewards, copies, other):
+    member = group_ids[0][:, None] == jnp.arange(GRP_ROW * copies, dtype=jnp.int32)[None, :]
+    sums = jnp.sum(jnp.where(member, rewards[0][:, None], 0.0), axis=0)
+    counts = jnp.sum(member.astype(jnp.float32), axis=0)
+    stats = jnp.concatenate([sums, counts])[None]
     vmem = pl.BlockSpec(memory_space=pltpu.VMEM)
     return pl.pallas_call(
-        stats_kernel,
-        in_specs=[vmem, vmem, pl.BlockSpec(memory_space=pl.ANY)],
+        spread_kernel,
+        in_specs=[vmem, pl.BlockSpec(memory_space=pl.ANY)],
         out_specs=vmem,
-        out_shape=jax.ShapeDtypeStruct((copies, 1, 2 * GRP_ROW * copies), rewards.dtype),
-    )(group_ids, rewards, other)
+        out_shape=jax.ShapeDtypeStruct((copies, *stats.shape), stats.dtype),
+    )(stats, other)
 
 
 def advantage_of(group_ids, rewards, stats):
@@ -205,7 +196,8 @@
         pair = jnp.stack([keys[0, :, cols], values[0, :, cols]])
         halos.append((shifted(pair, "ctx", 1), shifted(pair, "ctx", 2)))
 
-    starts = jnp.cumsum(lengths[0]) - lengths[0]
+    index = jnp.arange(lengths.shape[1], dtype=jnp.int32)
+    starts = jnp.sum(jnp.where(index[None, :] < index[:, None], lengths, 0), axis=1)
     first_row = lax.axis_index("ctx") * ROWS
     position = first_row + jnp.arange(ROWS, dtype=jnp.int32)
     begun = starts[None, :] <= position[:, None]

time: 68 us -> 70.9 us (1.043)
  waiting for transfers between devices: 7.33 us -> 10.9 us
  starting transfers between devices: 34.2 us -> 33.3 us
    ppermute x8, waiting for transfers between devices: 3.31 us -> 8.07 us  [shifted(): return lax.ppermute(x, axis, pairs)]
    all_to_all x1, waiting for transfers between devices: 4.02 us -> 2.79 us  [advantage_of(): lax.all_to_all(stats, 'grp', 0, 0, tiled=True)]
    ppermute x8, starting transfers between devices: 29.7 us -> 28.8 us  [shifted(): return lax.ppermute(x, axis, pairs)]
  transfers between devices with their start and end apart: 9 -> 9, of which waited for: 2 -> 3; matrix products, arithmetic and copies ran while one was open for 3% -> 4% of each run, Pallas kernels for 28% -> 27%
where the time goes in v5:
time: 70.9 us; the launch traced here: 70.4 us
  starting transfers between devices  33.3 us (47%)
  Pallas kernels  18.8 us (27%)
  waiting for transfers between devices  10.9 us (15%)
  other arithmetic  5.35 us (8%)
  local copies, waits for them, and re-layouts  1.3 us (2%)
  between operations  0.84 us (1%)
    ppermute x8, starting transfers between devices, shifted(): return lax.ppermute(x, axis, pairs)  28.8 us
    pallas_call x2, Pallas kernels, attention_backward(): pl.pallas_call(functools.partial(attention_kernel, ahead), grid=(groups,)...  17.6 us
    ppermute x8, waiting for transfers between devices, shifted(): return lax.ppermute(x, axis, pairs)  8.07 us
    all_to_all x1, starting transfers between devices, advantage_of(): lax.all_to_all(stats, 'grp', 0, 0, tiled=True)  4.47 us
    all_to_all x1, waiting for transfers between devices, advantage_of(): lax.all_to_all(stats, 'grp', 0, 0, tiled=True)  2.79 us
  transfers between devices with their start and end apart: 9, of which 3 were waited for; matrix products, arithmetic and copies ran while one was open for 4% of the time, Pallas kernels for 27%

profile of v5, /device:TPU:384, one launch (start us, length us, event | category | flops | bytes accessed | tf_op | source)
XLA Modules:
  0.0 70.4 jit_solution(9421076000248873498)
XLA Ops:
  0.7 1.2 %fusion.9 = (bf16[1,256,256]{2,1,0:T(8,128)(2,1)S(1)}, bf16[1,256,256]{2,1,0:T(8,128)(2,1)S(1)}, bf16[1,256,256]{2,1,0:T(8,128)(2,1)S(1)}, bf16[1,256,256]{2,1,0:T(8,128)(2,1)S(1)}) fusion(bf16[1,256,512]{2,1,0:T(8,128)(2,1)} %param.8, bf16[1,256,512]{2,1,0:T(8,128)(2,1)} %param.9), kind=kLoop, calls=%fused_computation.35 | loop fusion | bytes 1048576 | tf_op jit(solution)/shard_map/slice | solution.py:196
  1.9 4.9 %collective-permute-start = (bf16[2,256,256]{2,1,0:T(8,128)(2,1)S(1)}, bf16[2,256,256]{2,1,0:T(8,128)(2,1)S(1)}, u32[]{:S(2)}, u32[]{:S(2)}) collective-permute-start(bf16[2,256,256]{2,1,0:T(8,128)(2,1)S(1)} %pad_maximum_fusion.1), channel_id=1, source_target_pairs={{0,16},{8,24},{16,32},{24,40},{32,48},{40,56},{48,64},{56,72},{64,... | collective-permute-start | bytes 786440 | tf_op jit(solution)/shard_map/ppermute | solution.py:32
  6.9 2.5 %collective-permute-start.1 = (bf16[2,256,256]{2,1,0:T(8,128)(2,1)S(1)}, bf16[2,256,256]{2,1,0:T(8,128)(2,1)S(1)}, u32[]{:S(2)}, u32[]{:S(2)}) collective-permute-start(bf16[2,256,256]{2,1,0:T(8,128)(2,1)S(1)} %pad_maximum_fusion.1), channel_id=1, source_target_pairs={{0,8},{8,16},{16,24},{24,32},{32,40},{40,48},{48,56},{56,64},{64,7... | collective-permute-start | bytes 786440 | tf_op jit(solution)/shard_map/ppermute | solution.py:32
  9.4 0.7 %pad_maximum_fusion.2 = bf16[2,256,256]{2,1,0:T(8,128)(2,1)} fusion(bf16[1,256,256]{2,1,0:T(8,128)(2,1)S(1)} %get-tuple-element.36, bf16[1,256,256]{2,1,0:T(8,128)(2,1)S(1)} %get-tuple-element.29), kind=kLoop, calls=%fused_computation.13 | loop fusion | flops 131072 | bytes 524288 | tf_op jit(solution)/shard_map/stack | solution.py:196
  10.1 4.4 %collective-permute-start.2 = (bf16[2,256,256]{2,1,0:T(8,128)(2,1)}, bf16[2,256,256]{2,1,0:T(8,128)(2,1)S(1)}, u32[]{:S(2)}, u32[]{:S(2)}) collective-permute-start(bf16[2,256,256]{2,1,0:T(8,128)(2,1)} %pad_maximum_fusion.2), channel_id=1, source_target_pairs={{0,16},{8,24},{16,32},{24,40},{32,48},{40,56},{48,64},{56,72},{64,... | collective-permute-start | bytes 786440 | tf_op jit(solution)/shard_map/ppermute | solution.py:32
  14.5 3.4 %collective-permute-start.3 = (bf16[2,256,256]{2,1,0:T(8,128)(2,1)}, bf16[2,256,256]{2,1,0:T(8,128)(2,1)S(1)}, u32[]{:S(2)}, u32[]{:S(2)}) collective-permute-start(bf16[2,256,256]{2,1,0:T(8,128)(2,1)} %pad_maximum_fusion.2), channel_id=1, source_target_pairs={{0,8},{8,16},{16,24},{24,32},{32,40},{40,48},{48,56},{56,64},{64,7... | collective-permute-start | bytes 786440 | tf_op jit(solution)/shard_map/ppermute | solution.py:32
  17.9 0.1 select_reduce_fusion.1
  18.0 0.1 fusion.6
  18.1 0.1 select_reduce_fusion.4
  18.2 0.6 maximum_bitcast_fusion.x_ref
  18.8 0.0 collective-permute-done.refs_0_
  18.8 6.8 %collective-permute-done.1.refs_1_ = bf16[2,256,256]{2,1,0:T(8,128)(2,1)S(1)} collective-permute-done((bf16[2,256,256]{2,1,0:T(8,128)(2,1)S(1)}, bf16[2,256,256]{2,1,0:T(8,128)(2,1)S(1)}, u32[]{:S(2)}, u32[]{:S(2)}) %collective-permute-start.1) | collective-permute-done | bytes 262176 | tf_op jit(solution)/shard_map/ppermute | solution.py:32
  25.6 9.4 %shard_map.94 = (bf16[256,2560]{1,0:T(8,128)(2,1)S(1)}, f32[2,256,256]{2,1,0:T(8,128)S(1)}, bf16[2,256,256]{2,1,0:T(8,128)(2,1)}, bf16[2,256,256]{2,1,0:T(8,128)...) custom-call(bf16[2,256,256]{2,1,0:T(8,128)(2,1)S(1)} %collective-permute-done.refs_0_, ...), custom_call_target="tpu_custom_call" | custom-call | flops 8000000000 | bytes 4194304 | tf_op jit(solution)/shard_map/pallas_call | solution.py:124
  35.0 2.2 %collective-permute-start.4 = (bf16[2,256,256]{2,1,0:T(8,128)(2,1)S(1)}, bf16[2,256,256]{2,1,0:T(8,128)(2,1)}, u32[]{:S(2)}, u32[]{:S(2)}) collective-permute-start(bf16[2,256,256]{2,1,0:T(8,128)(2,1)S(1)} %get-tuple-element.17), channel_id=1, source_target_pairs={{16,0},{24,8},{32,16},{40,24},{48,32},{56,40},{64,48},{72,56},{80,... | collective-permute-start | bytes 786440 | tf_op jit(solution)/shard_map/ppermute | solution.py:32
  37.2 3.3 %collective-permute-start.5 = (bf16[2,256,256]{2,1,0:T(8,128)(2,1)}, bf16[2,256,256]{2,1,0:T(8,128)(2,1)}, u32[]{:S(2)}, u32[]{:S(2)}) collective-permute-start(bf16[2,256,256]{2,1,0:T(8,128)(2,1)} %get-tuple-element.19), channel_id=1, source_target_pairs={{8,0},{16,8},{24,16},{32,24},{40,32},{48,40},{56,48},{64,56},{72,6... | collective-permute-start | bytes 786440 | tf_op jit(solution)/shard_map/ppermute | solution.py:32
  40.5 0.0 collective-permute-done.3.refs_2_
  40.5 8.2 %shard_map.95 = (bf16[256,2560]{1,0:T(8,128)(2,1)S(1)}, f32[2,256,256]{2,1,0:T(8,128)S(1)}, bf16[2,256,256]{2,1,0:T(8,128)(2,1)}, bf16[2,256,256]{2,1,0:T(8,128)(2,1)}) custom-call(bf16[256,2560]{1,0:T(8,128)(2,1)S(1)} %get-tuple-element.13.refs_0_, bf16[2,256,256]{2,1,0:T(8,128)(2,1)S(1)} %collective-permute-done.2.refs_1_, ...), custom_call_target="tpu_custom_call", output_to_operand_aliasing={{0}: (0, {})} | custom-call | flops 8000000000 | bytes 4194304 | tf_op jit(solution)/shard_map/pallas_call | solution.py:124
  48.8 5.3 %collective-permute-start.6 = (bf16[2,256,256]{2,1,0:T(8,128)(2,1)}, bf16[2,256,256]{2,1,0:T(8,128)(2,1)S(1)}, u32[]{:S(2)}, u32[]{:S(2)}) collective-permute-start(bf16[2,256,256]{2,1,0:T(8,128)(2,1)} %get-tuple-element.21), channel_id=1, source_target_pairs={{16,0},{24,8},{32,16},{40,24},{48,32},{56,40},{64,48},{72,56},{80,... | collective-permute-start | bytes 786440 | tf_op jit(solution)/shard_map/ppermute | solution.py:32
  54.0 2.9 %collective-permute-start.7 = (bf16[2,256,256]{2,1,0:T(8,128)(2,1)}, bf16[2,256,256]{2,1,0:T(8,128)(2,1)S(1)}, u32[]{:S(2)}, u32[]{:S(2)}) collective-permute-start(bf16[2,256,256]{2,1,0:T(8,128)(2,1)} %get-tuple-element.22), channel_id=1, source_target_pairs={{8,0},{16,8},{24,16},{32,24},{40,32},{48,40},{56,48},{64,56},{72,6... | collective-permute-start | bytes 786440 | tf_op jit(solution)/shard_map/ppermute | solution.py:32
  56.9 0.0 collective-permute-done.4._
  56.9 1.2 %shard_map.96 = f32[8,1,64]{2,1,0:T(1,128)} custom-call(f32[1,64]{1,0:T(1,128)} %maximum_bitcast_fusion.x_ref, bf16[2,256,256]{2,1,0:T(8,128)(2,1)} %collective-permute-done.4._), custom_call_target="tpu_custom_call" | custom-call | tf_op jit(solution)/shard_map/pallas_call | solution.py:174
  58.1 4.5 %all-to-all-start = ((f32[8,1,64]{2,1,0:T(1,128)}), f32[8,1,64]{2,1,0:T(1,128)S(1)}, u32[]{:S(2)}, u32[]{:S(2)}) async-start(f32[8,1,64]{2,1,0:T(1,128)} %shard_map.96), calls=%async_computation | async-start | bytes 8192 | tf_op jit(solution)/shard_map/all_to_all | solution.py:183
  62.6 0.0 collective-permute-done.5
  62.6 1.1 %convert_add_fusion.1 = f32[2,256,256]{2,1,0:T(8,128)S(1)} fusion(bf16[2,256,256]{2,1,0:T(8,128)(2,1)} %collective-permute-done.5, f32[2,256,256]{2,1,0:T(8,128)S(1)} %get-tuple-element.18, bf16[2,256,256]{2,1,0:T(8,128)(2,1)} %collective-permute-done.4._), kind=kLoop, calls=%fused_computation.11 | loop fusion | flops 524288 | bytes 1572864 | tf_op jit(solution)/shard_map/add | solution.py:222
  63.7 1.3 %collective-permute-done.7 = bf16[2,256,256]{2,1,0:T(8,128)(2,1)S(1)} collective-permute-done((bf16[2,256,256]{2,1,0:T(8,128)(2,1)}, bf16[2,256,256]{2,1,0:T(8,128)(2,1)S(1)}, u32[]{:S(2)}, u32[]{:S(2)}) %collective-permute-start.7) | collective-permute-done | bytes 262176 | tf_op jit(solution)/shard_map/ppermute | solution.py:32
  65.0 0.1 convert_add_fusion
  65.1 2.8 %all-to-all-done = f32[8,1,64]{2,1,0:T(1,128)S(1)} async-done(((f32[8,1,64]{2,1,0:T(1,128)}), f32[8,1,64]{2,1,0:T(1,128)S(1)}, u32[]{:S(2)}, u32[]{:S(2)}) %all-to-all-start) | async-done | bytes 2080 | tf_op jit(solution)/shard_map/all_to_all | solution.py:183
  67.9 0.1 slice_bitcast_fusion
  68.0 0.1 select_reduce_fusion.3
  68.1 0.1 select_reduce_fusion
  68.2 1.3 %fusion = bf16[1,256,2560]{2,1,0:T(8,128)(2,1)} fusion(bf16[256,2560]{1,0:T(8,128)(2,1)S(1)} %get-tuple-element.16, f32[256]{0:T(256)S(1)} %broadcast_multiply_fusion), kind=kLoop, calls=%fused_computation.1 | loop fusion | flops 1966080 | bytes 2622464 | tf_op jit(solution)/shard_map/broadcast_in_dim | solution.py:226
  69.5 0.9 %fusion.5 = (bf16[1,256,512]{2,1,0:T(8,128)(2,1)}, bf16[1,256,512]{2,1,0:T(8,128)(2,1)}) fusion(f32[2,256,256]{2,1,0:T(8,128)S(1)} %convert_add_fusion, f32[2,256,256]{2,1,0:T(8,128)S(1)} %convert_add_fusion.1, f32[256]{0:T(256)S(1)} %select_reduce_fusion, f32[256]{0:T(256)S(1)} %broadcast_multiply_fusion), kind=kLoop, calls=%fused_computation.9 | loop fusion | flops 786432 | bytes 1574912 | tf_op jit(solution)/shard_map/convert_element_type | solution.py:225
  (18 shorter events, 0.1 us)
Async XLA Ops:
  0.6 25.0 %copy-start = (bf16[1,256,512]{2,1,0:T(8,128)(2,1)S(1)}, bf16[1,256,512]{2,1,0:T(8,128)(2,1)}, u32[]{:S(2)}) copy-start(bf16[1,256,512]{2,1,0:T(8,128)(2,1)} %param.8) | copy-start | bytes 786436
  0.6 25.0 %copy-start.1 = (bf16[1,256,512]{2,1,0:T(8,128)(2,1)S(1)}, bf16[1,256,512]{2,1,0:T(8,128)(2,1)}, u32[]{:S(2)}) copy-start(bf16[1,256,512]{2,1,0:T(8,128)(2,1)} %param.9) | copy-start | bytes 786436
  0.7 17.2 %copy-start.4 = (s32[1,64]{1,0:T(1,128)S(1)}, s32[1,64]{1,0:T(1,128)}, u32[]{:S(2)}) copy-start(s32[1,64]{1,0:T(1,128)} %param.11) | copy-start | bytes 772
  0.7 17.5 %copy-start.2 = (s32[1,64]{1,0:T(1,128)S(1)}, s32[1,64]{1,0:T(1,128)}, u32[]{:S(2)}) copy-start(s32[1,64]{1,0:T(1,128)} %param.12) | copy-start | bytes 772
  0.7 17.5 %copy-start.3 = (f32[1,64]{1,0:T(1,128)S(1)}, f32[1,64]{1,0:T(1,128)}, u32[]{:S(2)}) copy-start(f32[1,64]{1,0:T(1,128)} %param.13) | copy-start | bytes 772
  1.9 16.9 %collective-permute-start = (bf16[2,256,256]{2,1,0:T(8,128)(2,1)S(1)}, bf16[2,256,256]{2,1,0:T(8,128)(2,1)S(1)}, u32[]{:S(2)}, u32[]{:S(2)}) collective-permute-start(bf16[2,256,256]{2,1,0:T(8,128)(2,1)S(1)} %pad_maximum_fusion.1), channel_id=1, source_target_pairs={{0,16},{8,24},{16,32},{24,40},{32,48},{40,56},{48,64},{56,72},{64,... | collective-permute-start | bytes 786440 | tf_op jit(solution)/shard_map/ppermute | solution.py:32
  6.9 18.8 %collective-permute-start.1 = (bf16[2,256,256]{2,1,0:T(8,128)(2,1)S(1)}, bf16[2,256,256]{2,1,0:T(8,128)(2,1)S(1)}, u32[]{:S(2)}, u32[]{:S(2)}) collective-permute-start(bf16[2,256,256]{2,1,0:T(8,128)(2,1)S(1)} %pad_maximum_fusion.1), channel_id=1, source_target_pairs={{0,8},{8,16},{16,24},{24,32},{32,40},{40,48},{48,56},{56,64},{64,7... | collective-permute-start | bytes 786440 | tf_op jit(solution)/shard_map/ppermute | solution.py:32
  10.1 30.4 %collective-permute-start.2 = (bf16[2,256,256]{2,1,0:T(8,128)(2,1)}, bf16[2,256,256]{2,1,0:T(8,128)(2,1)S(1)}, u32[]{:S(2)}, u32[]{:S(2)}) collective-permute-start(bf16[2,256,256]{2,1,0:T(8,128)(2,1)} %pad_maximum_fusion.2), channel_id=1, source_target_pairs={{0,16},{8,24},{16,32},{24,40},{32,48},{40,56},{48,64},{56,72},{64,... | collective-permute-start | bytes 786440 | tf_op jit(solution)/shard_map/ppermute | solution.py:32
  14.5 26.1 %collective-permute-start.3 = (bf16[2,256,256]{2,1,0:T(8,128)(2,1)}, bf16[2,256,256]{2,1,0:T(8,128)(2,1)S(1)}, u32[]{:S(2)}, u32[]{:S(2)}) collective-permute-start(bf16[2,256,256]{2,1,0:T(8,128)(2,1)} %pad_maximum_fusion.2), channel_id=1, source_target_pairs={{0,8},{8,16},{16,24},{24,32},{32,40},{40,48},{48,56},{56,64},{64,7... | collective-permute-start | bytes 786440 | tf_op jit(solution)/shard_map/ppermute | solution.py:32
  35.0 21.9 %collective-permute-start.4 = (bf16[2,256,256]{2,1,0:T(8,128)(2,1)S(1)}, bf16[2,256,256]{2,1,0:T(8,128)(2,1)}, u32[]{:S(2)}, u32[]{:S(2)}) collective-permute-start(bf16[2,256,256]{2,1,0:T(8,128)(2,1)S(1)} %get-tuple-element.17), channel_id=1, source_target_pairs={{16,0},{24,8},{32,16},{40,24},{48,32},{56,40},{64,48},{72,56},{80,... | collective-permute-start | bytes 786440 | tf_op jit(solution)/shard_map/ppermute | solution.py:32
  37.2 25.4 %collective-permute-start.5 = (bf16[2,256,256]{2,1,0:T(8,128)(2,1)}, bf16[2,256,256]{2,1,0:T(8,128)(2,1)}, u32[]{:S(2)}, u32[]{:S(2)}) collective-permute-start(bf16[2,256,256]{2,1,0:T(8,128)(2,1)} %get-tuple-element.19), channel_id=1, source_target_pairs={{8,0},{16,8},{24,16},{32,24},{40,32},{48,40},{56,48},{64,56},{72,6... | collective-permute-start | bytes 786440 | tf_op jit(solution)/shard_map/ppermute | solution.py:32
  48.8 14.9 %collective-permute-start.6 = (bf16[2,256,256]{2,1,0:T(8,128)(2,1)}, bf16[2,256,256]{2,1,0:T(8,128)(2,1)S(1)}, u32[]{:S(2)}, u32[]{:S(2)}) collective-permute-start(bf16[2,256,256]{2,1,0:T(8,128)(2,1)} %get-tuple-element.21), channel_id=1, source_target_pairs={{16,0},{24,8},{32,16},{40,24},{48,32},{56,40},{64,48},{72,56},{80,... | collective-permute-start | bytes 786440 | tf_op jit(solution)/shard_map/ppermute | solution.py:32
  54.0 11.0 %collective-permute-start.7 = (bf16[2,256,256]{2,1,0:T(8,128)(2,1)}, bf16[2,256,256]{2,1,0:T(8,128)(2,1)S(1)}, u32[]{:S(2)}, u32[]{:S(2)}) collective-permute-start(bf16[2,256,256]{2,1,0:T(8,128)(2,1)} %get-tuple-element.22), channel_id=1, source_target_pairs={{8,0},{16,8},{24,16},{32,24},{40,32},{48,40},{56,48},{64,56},{72,6... | collective-permute-start | bytes 786440 | tf_op jit(solution)/shard_map/ppermute | solution.py:32
  58.1 9.7 %all-to-all-start = ((f32[8,1,64]{2,1,0:T(1,128)}), f32[8,1,64]{2,1,0:T(1,128)S(1)}, u32[]{:S(2)}, u32[]{:S(2)}) async-start(f32[8,1,64]{2,1,0:T(1,128)} %shard_map.96), calls=%async_computation | async-start | bytes 8192 | tf_op jit(solution)/shard_map/all_to_all | solution.py:183
